TPU v7x, 512 devices: a whole 4x4x16 slice. The times are simulated.
512 devices in a mesh: ctx: 64 (over z, y), tp: 8 (over x, core).
Axes of the slice: x: 4, y: 4, z: 16, core: 2. Of those that a mesh axis runs over, the one named last changes fastest.
Arguments:
- query_in: bfloat16 [16384, 8192], P('ctx', 'tp'), may hold values from -6 to 6
- key_in: bfloat16 [16384, 8192], P('ctx', 'tp'), may hold values from -6 to 6
- value_in: bfloat16 [16384, 8192], P('ctx', 'tp'), may hold values from -6 to 6
- out_grad: bfloat16 [16384, 8192], P('ctx', 'tp'), may hold values from -400 to 400
- fill_counts: int32 [64], P('ctx'), may hold values from 192 to 256, as said below
- doc_starts: int32 [4], replicated, may hold values from 0 to 12287, as said below
- feat_taps: bfloat16 [3, 7, 8192], P(None, None, 'tp'), may hold values from -2 to 2
- mix_taps: bfloat16 [512, 128], P('tp'), may hold values from -0.5 to 0.5
- skip_gain: float32 [8192], P('tp'), may hold values from -4 to 4
Outputs:
- hyena_out: bfloat16 [16384, 8192], P('ctx', 'tp')
- query_grad: bfloat16 [16384, 8192], P('ctx', 'tp')
- key_grad: bfloat16 [16384, 8192], P('ctx', 'tp')
- value_grad: bfloat16 [16384, 8192], P('ctx', 'tp')
- mix_grad: float32 [512, 128], P('tp')
- skip_grad: float32 [8192], P('tp')
- feat_grad: float32 [3, 7, 8192], P(None, None, 'tp')
Inputs may be any that keep to these rules, and one draw needn't show every extreme that they name: `fill_counts`: entry s is the number of filled slots of shard s; the filled slots are a shard's first ones. Some shard is full. `doc_starts`: strictly increasing; the first entry is 0.
All inputs are finite; a program needn't handle non-finite values.
Results may differ from a plain program's by a relative error of at most 0.0075.
Values may be sent and summed in bfloat16 or wider, within the bound.
A program may use at most 128 MiB of HBM per device.

v0:
```python
import math

import jax
import jax.numpy as jnp
from jax import lax
from jax.sharding import PartitionSpec as P


def prefix(value, axis, join, neutral):
    count, mine = (lax.axis_size(axis), lax.axis_index(axis))
    pieces = lax.all_gather(value, axis)
    so_far = jnp.full_like(value, 0) + jnp.asarray(neutral, value.dtype)

    def turn(position, so_far):
        longer = join(so_far, pieces[position])
        return jnp.where(position < mine, longer, so_far)

    return lax.fori_loop(0, count - 1, turn, so_far)


def from_behind(value, axis, steps):
    count = lax.axis_size(axis)
    leading, last = (max(0, -steps), min(count, count - steps))
    return lax.ppermute(value, axis, [(source, source + steps) for source in range(leading, last)])


def doc_index(positions, doc_starts):
    counted = jnp.sum((doc_starts[None, :] <= positions[:, None]).astype(jnp.int32), axis=1)
    return counted - 1


def banded(coeffs, block_rows):
    group_count, filter_len = coeffs.shape
    window = block_rows + filter_len - 1
    padded_row = jnp.concatenate(
        [coeffs, jnp.zeros((group_count, window + 1 - filter_len), coeffs.dtype)], axis=1
    )
    tiled = jnp.broadcast_to(padded_row[:, None, :], (group_count, block_rows, window + 1))
    tiled = tiled.reshape(group_count, block_rows * (window + 1))
    return tiled[:, : block_rows * window].reshape(group_count, block_rows, window)


def diagonals(products, filter_len):
    group_count, block_rows, window = products.shape
    flat = jnp.concatenate(
        [
            products.reshape(group_count, block_rows * window),
            jnp.zeros((group_count, block_rows), products.dtype),
        ],
        axis=1,
    )
    return jnp.sum(flat.reshape(group_count, block_rows, window + 1)[:, :, :filter_len], axis=1)


def contract(form, left, right):
    return jnp.einsum(form, left, right, preferred_element_type=jnp.float32)


def featurize(extended, doc_ext, weights):
    short_len = weights.shape[0]
    out_rows = extended.shape[0] - short_len + 1
    doc_out = doc_ext[short_len - 1 :]
    accum = jnp.zeros((out_rows, extended.shape[1]), jnp.float32)
    for j in range(short_len):
        offset = short_len - 1 - j
        source = extended[offset : offset + out_rows].astype(jnp.float32)
        same_doc = (doc_out == doc_ext[offset : offset + out_rows])[:, None]
        accum = accum + jnp.where(same_doc, weights[j].astype(jnp.float32) * source, 0.0)
    return accum


def unfeaturize(extended, doc_ext, weights):
    short_len = weights.shape[0]
    out_rows = extended.shape[0] - short_len + 1
    doc_out = doc_ext[:out_rows]
    accum = jnp.zeros((out_rows, extended.shape[1]), jnp.float32)
    for j in range(short_len):
        source = extended[j : j + out_rows].astype(jnp.float32)
        same_doc = (doc_out == doc_ext[j : j + out_rows])[:, None]
        accum = accum + jnp.where(same_doc, weights[j].astype(jnp.float32) * source, 0.0)
    return accum


def feat_grads(extended, doc_ext, grads):
    out_rows = grads.shape[0]
    short_len = extended.shape[0] - out_rows + 1
    doc_out = doc_ext[short_len - 1 :]
    pieces = []
    for j in range(short_len):
        offset = short_len - 1 - j
        source = extended[offset : offset + out_rows].astype(jnp.float32)
        same_doc = (doc_out == doc_ext[offset : offset + out_rows])[:, None]
        pieces.append(jnp.sum(jnp.where(same_doc, source * grads.astype(jnp.float32), 0.0), axis=0))
    return jnp.stack(pieces)


def mix_blocks(extended, doc_ext, band):
    group_count, block_rows, window = band.shape
    filter_len = window - block_rows + 1
    channels = extended.shape[1]
    per_group = channels // group_count
    out_rows = extended.shape[0] - filter_len + 1

    def mix_per_block(b):
        first = b * block_rows
        source = lax.dynamic_slice_in_dim(extended, first, window, 0).reshape(
            window, group_count, per_group
        )
        doc_src = lax.dynamic_slice_in_dim(doc_ext, first, window, 0)
        doc_out = doc_src[filter_len - 1 :]
        matrix = jnp.where(
            (doc_out[:, None] == doc_src[None, :])[None], band, jnp.zeros((), band.dtype)
        )
        return contract("gas,sgc->agc", matrix, source).reshape(block_rows, channels)

    blocks = lax.map(mix_per_block, jnp.arange(out_rows // block_rows, dtype=jnp.int32))
    return blocks.reshape(out_rows, channels)


def grad_blocks(ext_grad, doc_back, ext_mix, doc_long, row_grads, band):
    group_count, block_rows, window = band.shape
    filter_len = window - block_rows + 1
    out_rows, channels = row_grads.shape
    per_group = channels // group_count

    def grad_per_block(b):
        first = b * block_rows
        source = lax.dynamic_slice_in_dim(ext_grad, first, window, 0).reshape(
            window, group_count, per_group
        )
        doc_src = lax.dynamic_slice_in_dim(doc_back, first, window, 0)
        matrix = jnp.where(
            (doc_src[:block_rows, None] == doc_src[None, :])[None], band, jnp.zeros((), band.dtype)
        )
        back_rows = contract("gas,sgc->agc", matrix, source).reshape(block_rows, channels)
        mix_src = lax.dynamic_slice_in_dim(ext_mix, first, window, 0).reshape(
            window, group_count, per_group
        )
        doc_mix = lax.dynamic_slice_in_dim(doc_long, first, window, 0)
        own_rows = lax.dynamic_slice_in_dim(row_grads, first, block_rows, 0).reshape(
            block_rows, group_count, per_group
        )
        products = contract("agc,sgc->gas", own_rows, mix_src)
        products = jnp.where(
            (doc_mix[filter_len - 1 :, None] == doc_mix[None, :])[None], products, 0.0
        )
        return (back_rows, diagonals(products, filter_len))

    back_all, taps_all = lax.map(
        grad_per_block, jnp.arange(out_rows // block_rows, dtype=jnp.int32)
    )
    return (back_all.reshape(out_rows, channels), jnp.sum(taps_all, axis=0)[:, ::-1])


def add_counts(earlier, later_part):
    return earlier + later_part


def shards(
    query_in, key_in, value_in, out_grad, fill_counts, doc_starts, feat_taps, mix_taps, skip_gain
):
    row_count, channels = query_in.shape
    short_len = feat_taps.shape[1]
    group_count, filter_len = mix_taps.shape
    block_rows = math.gcd(row_count, 128)
    filled = fill_counts[0]
    offsets = prefix(fill_counts, "ctx", add_counts, jnp.zeros((1,), jnp.int32))
    first_pos = offsets[0]
    slot_pos = jnp.arange(row_count, dtype=jnp.int32)
    is_valid = (slot_pos < filled)[:, None]

    def tail_rows(source, count):
        return lax.dynamic_slice_in_dim(source, filled - count, count, 0)

    prev_short = from_behind(
        (
            tail_rows(query_in, short_len - 1),
            tail_rows(key_in, short_len - 1),
            tail_rows(value_in, short_len - 1),
        ),
        "ctx",
        1,
    )
    doc_short = doc_index(
        first_pos - short_len + 1 + jnp.arange(row_count + short_len - 1, dtype=jnp.int32),
        doc_starts,
    )
    ext_q = jnp.concatenate([prev_short[0], query_in], axis=0)
    ext_k = jnp.concatenate([prev_short[1], key_in], axis=0)
    ext_v = jnp.concatenate([prev_short[2], value_in], axis=0)
    query = featurize(ext_q, doc_short, feat_taps[0])
    keys = featurize(ext_k, doc_short, feat_taps[1])
    values = featurize(ext_v, doc_short, feat_taps[2])
    mix_in = (keys * values).astype(jnp.bfloat16)
    prev_mix = from_behind(tail_rows(mix_in, filter_len - 1), "ctx", 1)
    ext_mix = jnp.concatenate([prev_mix, mix_in], axis=0)
    doc_long = doc_index(
        first_pos - filter_len + 1 + jnp.arange(row_count + filter_len - 1, dtype=jnp.int32),
        doc_starts,
    )
    mixed = mix_blocks(ext_mix, doc_long, banded(mix_taps[:, ::-1], block_rows))
    gated = mixed + skip_gain[None, :] * mix_in.astype(jnp.float32)
    hyena_out = jnp.where(is_valid, query * gated, 0.0).astype(jnp.bfloat16)
    grad_f = out_grad.astype(jnp.float32)
    mix_grad_rows = jnp.where(is_valid, grad_f * query, 0.0).astype(jnp.bfloat16)
    query_back = jnp.where(is_valid, grad_f * gated, 0.0).astype(jnp.bfloat16)
    next_mix = from_behind(mix_grad_rows[: filter_len - 1], "ctx", -1)
    ext_grad = jnp.concatenate(
        [mix_grad_rows, jnp.zeros((filter_len - 1, channels), jnp.bfloat16)], axis=0
    )
    ext_grad = lax.dynamic_update_slice_in_dim(ext_grad, next_mix, filled, 0)
    doc_back = doc_index(
        first_pos + jnp.arange(row_count + filter_len - 1, dtype=jnp.int32), doc_starts
    )
    back_rows, taps_grad = grad_blocks(
        ext_grad, doc_back, ext_mix, doc_long, mix_grad_rows, banded(mix_taps, block_rows)
    )
    mix_back = back_rows + skip_gain[None, :] * mix_grad_rows.astype(jnp.float32)
    key_back = jnp.where(is_valid, mix_back * values, 0.0).astype(jnp.bfloat16)
    value_back = jnp.where(is_valid, mix_back * keys, 0.0).astype(jnp.bfloat16)
    next_grads = from_behind(
        (query_back[: short_len - 1], key_back[: short_len - 1], value_back[: short_len - 1]),
        "ctx",
        -1,
    )
    doc_near = doc_back[: row_count + short_len - 1]
    tail_pad = jnp.zeros((short_len - 1, channels), jnp.bfloat16)
    in_grads = []
    for which, back_part in enumerate((query_back, key_back, value_back)):
        extended = lax.dynamic_update_slice_in_dim(
            jnp.concatenate([back_part, tail_pad], axis=0), next_grads[which], filled, 0
        )
        in_grads.append(
            jnp.where(is_valid, unfeaturize(extended, doc_near, feat_taps[which]), 0.0).astype(
                jnp.bfloat16
            )
        )
    feat = jnp.stack(
        [
            feat_grads(ext_q, doc_short, query_back),
            feat_grads(ext_k, doc_short, key_back),
            feat_grads(ext_v, doc_short, value_back),
        ]
    )
    skip_part = jnp.sum(mix_in.astype(jnp.float32) * mix_grad_rows.astype(jnp.float32), axis=0)
    total_params = (group_count * filter_len + channels * (1 + 3 * short_len)) * lax.axis_size("tp")
    taps_sum, skip_sum, feat_sum = lax.psum((taps_grad, skip_part, feat), "ctx")
    local_sq = (
        jnp.sum(taps_sum * taps_sum) + jnp.sum(skip_sum * skip_sum) + jnp.sum(feat_sum * feat_sum)
    )
    whole_sq = lax.psum(local_sq, "tp")
    factor = lax.rsqrt(whole_sq / total_params + 1e-06)
    mix_out = taps_sum * factor
    skip_out = skip_sum * factor
    feat_out = feat_sum * factor
    return (hyena_out, in_grads[0], in_grads[1], in_grads[2], mix_out, skip_out, feat_out)


def solution(mesh):
    in_specs = (
        P("ctx", "tp"),
        P("ctx", "tp"),
        P("ctx", "tp"),
        P("ctx", "tp"),
        P("ctx"),
        P(),
        P(None, None, "tp"),
        P("tp", None),
        P("tp"),
    )
    out_specs = (
        P("ctx", "tp"),
        P("ctx", "tp"),
        P("ctx", "tp"),
        P("ctx", "tp"),
        P("tp", None),
        P("tp"),
        P(None, None, "tp"),
    )
    return jax.shard_map(shards, mesh=mesh, in_specs=in_specs, out_specs=out_specs, check_vma=False)
```

profile of v0, /device:TPU:1, one launch (start us, length us, event | category | flops | bytes accessed | tf_op | source)
XLA Modules:
  0.0 870.6 jit_solution(18303763813222959009)
XLA Ops:
  8.6 4.0 collective-permute-start.2
  13.5 3.2 collective-permute-start.1
  17.4 2.9 collective-permute-start
  22.4 26.5 %all-reduce.7 = s32[64]{0:T(128)S(1)} all-reduce(s32[64]{0:T(128)S(1)} %dynamic-update-slice), channel_id=2, replica_groups=mesh['ctx'=64,'tp'=8] {'ctx'}, use_global_device_ids=true, to_apply=%add.7 | all-reduce | flops 64 | bytes 512
  48.9 79.7 %while.35 = (s32[]{:T(128)}, s32[1]{0:T(128)}, s32[]{:T(128)}, s32[64,1]{0,1:T(1,128)S(1)}, s32[]{:T(128)}) while((s32[]{:T(128)}, s32[1]{0:T(128)}, s32[]{:T(128)}, s32[64,1]{0,1:T(1,128)S(1)}, s32[]{:T(128)}) %tuple.131), condition=%wide.region_1.2_spmd, body=%wide.region_0.1_spmd.sunk | while | flops 5 | bytes 115 | solution.py:18
  132.4 13.3 %fusion.52 = (f32[1024]{0:T(1024)}, bf16[256,1024]{1,0:T(8,128)(2,1)S(1)}, bf16[256,1024]{1,0:T(8,128)(2,1)S(1)}, f32[256,1024]{1,0:T(8,128)}, f32[256,1024]{1,0:T(8,128)}, /*index=5*/f32[256,1024]{1,0:T(8,128)}) fusion(bf16[256,1024]{1,0:T(8,128)(2,1)} %param.18, pred[256]{0:T(512)(128)(4,1)S(1)} %iota_compare_fusion, bf16[256,1024]{1,0:T(8,128)(2,1)} %param.17, ...), kind=kLoop, calls=%fused_computation.127 | loop fusion | flops 37223424 | bytes 6420224 | tf_op jit(solution)/shard_map/reduce_sum | solution.py:245
  148.6 2.6 copy.68
  153.5 15.8 %reshape.367 = bf16[64,128,255]{2,1,0:T(8,128)(2,1)} reshape(bf16[64,32640]{1,0:T(8,128)(2,1)} %slice.526) | data formatting | bytes 8355840 | tf_op jit(solution)/shard_map/reshape | solution.py:40
  169.6 2.6 copy.67
  174.4 15.8 %reshape.364 = bf16[64,128,255]{2,1,0:T(8,128)(2,1)} reshape(bf16[64,32640]{1,0:T(8,128)(2,1)} %slice.516) | data formatting | bytes 8355840 | tf_op jit(solution)/shard_map/reshape | solution.py:40
  194.9 12.3 %while.36 = (s32[]{:T(128)}, f32[2,128,1024]{2,1,0:T(8,128)}, s32[2]{0:T(128)S(1)}, bf16[383,1024]{0,1:T(8,128)(2,1)S(1)}, s32[383]{0:T(512)S(1)}, /*index=5*/bf...) while((s32[]{:T(128)}, f32[2,128,1024]{2,1,0:T(8,128)}, s32[2]{0:T(128)S(1)}, ...), condition=%wide.region_5.6_spmd, body=%wide.region_4.5_spmd.sunk | while | flops 68968328 | bytes 8436135 | solution.py:116
  196.6 3.4 fusion.126
  202.8 3.4 fusion.126
  207.3 6.2 fusion.65
  218.4 2.5 dynamic_update_slice.24
  222.5 64.3 %while.37 = (s32[]{:T(128)}, f32[2,128,1024]{2,1,0:T(8,128)}, f32[2,64,128]{2,1,0:T(8,128)}, s32[2]{0:T(128)}, bf16[383,1024]{1,0:T(8,128)(2,1)S(1)}, /*index=5*...) while((s32[]{:T(128)}, f32[2,128,1024]{2,1,0:T(8,128)}, ...), condition=%wide.region_9.10_spmd, body=%wide.region_7.9_spmd.sunk | while | flops 138977024 | bytes 75834160 | solution.py:149
  226.4 4.3 fusion.131
  232.8 4.5 broadcast_select_fusion.2
  237.3 9.3 %reshape.397 = f32[64,32640]{1,0:T(8,128)} reshape(f32[64,128,255]{2,1,0:T(8,128)} %broadcast_select_fusion.2) | data formatting | bytes 16711680 | tf_op jit(solution)/shard_map/while/body/eval_jaxpr/reshape | solution.py:47
  246.6 4.0 concatenate.44
  250.7 2.5 copy.78
  258.5 4.3 fusion.131
  265.0 4.5 broadcast_select_fusion.2
  269.5 9.3 %reshape.397 = f32[64,32640]{1,0:T(8,128)} reshape(f32[64,128,255]{2,1,0:T(8,128)} %broadcast_select_fusion.2) | data formatting | bytes 16711680 | tf_op jit(solution)/shard_map/while/body/eval_jaxpr/reshape | solution.py:47
  278.7 4.0 concatenate.44
  282.8 2.5 copy.78
  287.9 223.1 %all-reduce.8 = (f32[64,128]{1,0:T(8,128)S(1)}, f32[1024]{0:T(1024)S(1)}) all-reduce(f32[64,128]{1,0:T(8,128)S(1)} %rev.7, f32[1024]{0:T(1024)} %get-tuple-element.288), channel_id=1, replica_groups=mesh['ctx'=64,'tp'=8] {'ctx'}, use_global_device_ids=true, to_apply=%region_11.12 | all-reduce | flops 9216 | bytes 73728 | tf_op jit(solution)/shard_map/psum | solution.py:247
  511.6 5.3 fusion.78
  527.1 2.3 select_convert_fusion.4
  529.7 2.3 select_convert_fusion
  532.2 301.2 %all-reduce.11.cloned.1.call-done = f32[3,7,1024]{2,1,0:T(8,128)} async-done(((f32[3,7,1024]{2,1,0:T(8,128)}), f32[3,7,1024]{2,1,0:T(8,128)}) %all-reduce.11.cloned.1.call-update) | async-done | bytes 86032 | tf_op jit(solution)/shard_map/psum | solution.py:247
  838.0 23.3 %psum.31 = f32[]{:T(128)} all-reduce(f32[]{:T(128)S(6)} %add.310), channel_id=1, replica_groups=mesh['ctx'=64,'tp'=8] {'tp'}, use_global_device_ids=true, to_apply=%region_39.40 | all-reduce | flops 1 | bytes 8 | tf_op jit(solution)/shard_map/psum | solution.py:251
  (320 shorter events, 97.4 us)
Async XLA Ops:
  7.2 141.0 %copy-start.11 = (bf16[64,128]{1,0:T(8,128)(2,1)S(1)}, bf16[64,128]{1,0:T(8,128)(2,1)}, u32[]{:S(2)}) copy-start(bf16[64,128]{1,0:T(8,128)(2,1)} %param.22) | copy-start | bytes 49156
  7.2 826.2 %all-reduce.11.cloned.1.call-start = ((), (), s32[]{:S(2)}) async-start(), calls=%async_computation | async-start | bytes 196608 | tf_op jit(solution)/shard_map/psum | solution.py:247
  8.6 123.8 %collective-permute-start.2 = (bf16[6,1024]{1,0:T(8,128)(2,1)S(1)}, bf16[6,1024]{1,0:T(8,128)(2,1)S(1)}, u32[]{:S(2)}, u32[]{:S(2)}) collective-permute-start(bf16[6,1024]{1,0:T(8,128)(2,1)S(1)} %constant_dynamic-slice_fusion.6), channel_id=1, source_target_pairs={{0,8},{8,16},{16,24},{24,32},{32,40},{40,48},{48,56},{56,64},{64,7... | collective-permute-start | bytes 36872 | tf_op jit(solution)/shard_map/ppermute | solution.py:24
  13.5 119.0 %collective-permute-start.1 = (bf16[6,1024]{1,0:T(8,128)(2,1)S(1)}, bf16[6,1024]{1,0:T(8,128)(2,1)S(1)}, u32[]{:S(2)}, u32[]{:S(2)}) collective-permute-start(bf16[6,1024]{1,0:T(8,128)(2,1)S(1)} %constant_dynamic-slice_fusion.7), channel_id=1, source_target_pairs={{0,8},{8,16},{16,24},{24,32},{32,40},{40,48},{48,56},{56,64},{64,7... | collective-permute-start | bytes 36872 | tf_op jit(solution)/shard_map/ppermute | solution.py:24
  17.4 115.0 %collective-permute-start = (bf16[6,1024]{1,0:T(8,128)(2,1)S(1)}, bf16[6,1024]{1,0:T(8,128)(2,1)S(1)}, u32[]{:S(2)}, u32[]{:S(2)}) collective-permute-start(bf16[6,1024]{1,0:T(8,128)(2,1)S(1)} %constant_dynamic-slice_fusion.8), channel_id=1, source_target_pairs={{0,8},{8,16},{16,24},{24,32},{32,40},{40,48},{48,56},{56,64},{64,7... | collective-permute-start | bytes 36872 | tf_op jit(solution)/shard_map/ppermute | solution.py:24
  129.4 19.1 %copy-start.34 = (f32[1,1,1024]{2,1,0:T(1,128)}, f32[1,1,1024]{2,1,0:T(1,128)S(1)}, u32[]{:S(2)}) copy-start(f32[1,1,1024]{2,1,0:T(1,128)S(1)} %get-tuple-element.313) | copy-start | bytes 12292
  129.4 19.1 %copy-start.36 = (f32[1,1,1024]{2,1,0:T(1,128)}, f32[1,1,1024]{2,1,0:T(1,128)S(1)}, u32[]{:S(2)}) copy-start(f32[1,1,1024]{2,1,0:T(1,128)S(1)} %get-tuple-element.314) | copy-start | bytes 12292
  130.7 17.9 %copy-start.14 = (f32[1,1,1024]{2,1,0:T(1,128)}, f32[1,1,1024]{2,1,0:T(1,128)S(1)}, u32[]{:S(2)}) copy-start(f32[1,1,1024]{2,1,0:T(1,128)S(1)} %get-tuple-element.297) | copy-start | bytes 12292
  130.7 17.9 %copy-start.22 = (f32[1,1,1024]{2,1,0:T(1,128)}, f32[1,1,1024]{2,1,0:T(1,128)S(1)}, u32[]{:S(2)}) copy-start(f32[1,1,1024]{2,1,0:T(1,128)S(1)} %get-tuple-element.307) | copy-start | bytes 12292
  131.6 75.7 %copy-start.47 = (pred[256]{0:T(512)(128)(4,1)}, pred[256]{0:T(512)(128)(4,1)S(1)}, u32[]{:S(2)}) copy-start(pred[256]{0:T(512)(128)(4,1)S(1)} %get-tuple-element.321) | copy-start | bytes 772
  131.6 75.7 %copy-start.49 = (pred[256]{0:T(512)(128)(4,1)}, pred[256]{0:T(512)(128)(4,1)S(1)}, u32[]{:S(2)}) copy-start(pred[256]{0:T(512)(128)(4,1)S(1)} %get-tuple-element.322) | copy-start | bytes 772
  131.6 75.7 %copy-start.51 = (pred[256]{0:T(512)(128)(4,1)}, pred[256]{0:T(512)(128)(4,1)S(1)}, u32[]{:S(2)}) copy-start(pred[256]{0:T(512)(128)(4,1)S(1)} %get-tuple-element.323) | copy-start | bytes 772
  131.6 75.7 %copy-start.53 = (pred[256]{0:T(512)(128)(4,1)}, pred[256]{0:T(512)(128)(4,1)S(1)}, u32[]{:S(2)}) copy-start(pred[256]{0:T(512)(128)(4,1)S(1)} %get-tuple-element.324) | copy-start | bytes 772
  131.6 75.7 %copy-start.55 = (pred[256]{0:T(512)(128)(4,1)}, pred[256]{0:T(512)(128)(4,1)S(1)}, u32[]{:S(2)}) copy-start(pred[256]{0:T(512)(128)(4,1)S(1)} %get-tuple-element.325) | copy-start | bytes 772
  131.6 75.7 %copy-start.57 = (pred[256]{0:T(512)(128)(4,1)}, pred[256]{0:T(512)(128)(4,1)S(1)}, u32[]{:S(2)}) copy-start(pred[256]{0:T(512)(128)(4,1)S(1)} %get-tuple-element.326) | copy-start | bytes 772
  132.4 84.9 %copy-start.38 = (pred[256]{0:T(512)(128)(4,1)}, pred[256]{0:T(512)(128)(4,1)S(1)}, u32[]{:S(2)}) copy-start(pred[256]{0:T(512)(128)(4,1)S(1)} %iota_compare_fusion) | copy-start | bytes 772
  145.7 47.5 %copy-start = (bf16[256,1024]{1,0:T(8,128)(2,1)}, bf16[256,1024]{1,0:T(8,128)(2,1)S(1)}, u32[]{:S(2)}) copy-start(bf16[256,1024]{1,0:T(8,128)(2,1)S(1)} %get-tuple-element.290) | copy-start | bytes 1572868
  145.8 47.4 %collective-permute-start.3 = (bf16[127,1024]{1,0:T(8,128)(2,1)S(1)}, bf16[127,1024]{1,0:T(8,128)(2,1)S(1)}, u32[]{:S(2)}, u32[]{:S(2)}) collective-permute-start(bf16[127,1024]{1,0:T(8,128)(2,1)S(1)} %constant_dynamic-slice_fusion.5), channel_id=1, source_target_pairs={{0,8},{8,16},{16,24},{24,32},{32,40},{40,48},{48,56},{56,64},{64,7... | collective-permute-start | bytes 780296 | tf_op jit(solution)/shard_map/ppermute | solution.py:24
  191.7 26.6 %collective-permute-start.5 = (bf16[127,1024]{1,0:T(8,128)(2,1)}, bf16[127,1024]{1,0:T(8,128)(2,1)}, u32[]{:S(2)}, u32[]{:S(2)}) collective-permute-start(bf16[127,1024]{1,0:T(8,128)(2,1)} %slice.525), channel_id=1, source_target_pairs={{8,0},{16,8},{24,16},{32,24},{40,32},{48,40},{56,48},{64,56},{72,6... | collective-permute-start | bytes 780296 | tf_op jit(solution)/shard_map/ppermute | solution.py:24
  216.0 310.0 %collective-permute-start.4 = (bf16[6,1024]{1,0:T(8,128)(2,1)}, bf16[6,1024]{1,0:T(8,128)(2,1)}, u32[]{:S(2)}, u32[]{:S(2)}) collective-permute-start(bf16[6,1024]{1,0:T(8,128)(2,1)} %slice.517), channel_id=1, source_target_pairs={{8,0},{16,8},{24,16},{32,24},{40,32},{48,40},{56,48},{64,56},{72,6... | collective-permute-start | bytes 36872 | tf_op jit(solution)/shard_map/ppermute | solution.py:24
  286.8 230.1 %copy-start.5 = (bf16[256,1024]{1,0:T(8,128)(2,1)S(1)}, bf16[256,1024]{1,0:T(8,128)(2,1)}, u32[]{:S(2)}) copy-start(bf16[256,1024]{1,0:T(8,128)(2,1)} %param.16) | copy-start | bytes 1572868
  286.8 230.3 %copy-start.2 = (f32[2,128,1024]{2,1,0:T(8,128)S(1)}, f32[2,128,1024]{2,1,0:T(8,128)}, u32[]{:S(2)}) copy-start(f32[2,128,1024]{2,1,0:T(8,128)} %get-tuple-element.173) | copy-start | bytes 3145732
  286.8 230.3 %copy-start.39 = (pred[256]{0:T(512)(128)(4,1)S(1)}, pred[256]{0:T(512)(128)(4,1)}, u32[]{:S(2)}) copy-start(pred[256]{0:T(512)(128)(4,1)} %copy-done.38) | copy-start | bytes 772
  286.8 230.4 %copy-start.48 = (pred[256]{0:T(512)(128)(4,1)S(1)}, pred[256]{0:T(512)(128)(4,1)}, u32[]{:S(2)}) copy-start(pred[256]{0:T(512)(128)(4,1)} %copy-done.47) | copy-start | bytes 772
  286.8 230.4 %copy-start.50 = (pred[256]{0:T(512)(128)(4,1)S(1)}, pred[256]{0:T(512)(128)(4,1)}, u32[]{:S(2)}) copy-start(pred[256]{0:T(512)(128)(4,1)} %copy-done.49) | copy-start | bytes 772
  286.8 230.4 %copy-start.52 = (pred[256]{0:T(512)(128)(4,1)S(1)}, pred[256]{0:T(512)(128)(4,1)}, u32[]{:S(2)}) copy-start(pred[256]{0:T(512)(128)(4,1)} %copy-done.51) | copy-start | bytes 772
  286.8 230.4 %copy-start.54 = (pred[256]{0:T(512)(128)(4,1)S(1)}, pred[256]{0:T(512)(128)(4,1)}, u32[]{:S(2)}) copy-start(pred[256]{0:T(512)(128)(4,1)} %copy-done.53) | copy-start | bytes 772
  286.8 230.4 %copy-start.56 = (pred[256]{0:T(512)(128)(4,1)S(1)}, pred[256]{0:T(512)(128)(4,1)}, u32[]{:S(2)}) copy-start(pred[256]{0:T(512)(128)(4,1)} %copy-done.55) | copy-start | bytes 772
  286.8 230.4 %copy-start.58 = (pred[256]{0:T(512)(128)(4,1)S(1)}, pred[256]{0:T(512)(128)(4,1)}, u32[]{:S(2)}) copy-start(pred[256]{0:T(512)(128)(4,1)} %copy-done.57) | copy-start | bytes 772
  522.2 7.3 collective-permute-start.7
  523.5 8.5 collective-permute-start.6
  833.4 29.7 %copy-start.9 = (f32[3,7,1024]{2,1,0:T(8,128)S(1)}, f32[3,7,1024]{2,1,0:T(8,128)}, u32[]{:S(2)}) copy-start(f32[3,7,1024]{2,1,0:T(8,128)} %all-reduce.11.cloned.1.call-done) | copy-start | bytes 258052
  (44 other events, 438.2 us)
Sparse Core Ops, SparseCore 0:
  522.3 311.0 all-reduce.10
where the time goes:
time: 874 us; the launch traced here: 871 us
  waiting for transfers between devices  301 us (34%)
  blocking collectives  273 us (31%)
  local copies, waits for them, and re-layouts  141 us (16%)
  other arithmetic  49.1 us (6%)
  loops' own time  45.7 us (5%)
  matrix products  24.5 us (3%)
  between operations  18.5 us (2%)
  starting transfers between devices  17.8 us (2%)
    psum x1, waiting for transfers between devices, shards(): taps_sum, skip_sum, feat_sum = lax.psum((taps_grad, skip_part, feat), 'ctx')  301 us
    psum x1, blocking collectives, shards(): taps_sum, skip_sum, feat_sum = lax.psum((taps_grad, skip_part, feat), 'ctx')  223 us
    another operation x1, loops' own time, prefix(): return lax.fori_loop(0, count - 1, turn, so_far)  42.9 us
    dynamic_slice x63, local copies, waits for them, and re-layouts, turn(): longer = join(so_far, pieces[position])  36.8 us
    reshape x2, local copies, waits for them, and re-layouts, banded(): tiled[:, :block_rows * window].reshape(group_count, block_rows, window)  31.7 us
    unnamed x1, blocking collectives  26.5 us
    dot_general x6, matrix products, contract(): return jnp.einsum(form, left, right, preferred_element_type=jnp.float32)  24.5 us
    psum x1, blocking collectives, shards(): whole_sq = lax.psum(local_sq, 'tp')  23.3 us
  transfers between devices with their start and end apart: 9, of which 1 were waited for; matrix products, arithmetic and copies ran while one was open for 22% of the time, Pallas kernels for 0%

commit v1 on v0

v1 whole, which is shorter than its diff:
```python
import jax
import jax.numpy as jnp
from jax import lax
from jax.experimental import pallas as pl
from jax.experimental.pallas import tpu as pltpu
from jax.sharding import PartitionSpec as P

F32 = jnp.float32
BF16 = jnp.bfloat16
I32 = jnp.int32
MESH = pl.DeviceIdType.MESH

NY = 4
HALO = 144
NEAR = 16
LANES = 128
SHORT = 7
FILT = 128
GROUP = 16
BIG = 1 << 28


def halo_kernel(nz, fill_ref, q_ref, k_ref, v_ref, g_ref, first_ref, from_prev, from_next,
                vbuf, tails, counts, load_sem, ysend, yrecv, zsend, zrecv, hsend, hrecv):
    me = lax.axis_index("ctx")
    z, y = me // NY, me % NY
    n = nz * NY
    nxt, prv = lax.rem(me + 1, n), lax.rem(me + n - 1, n)
    rows = q_ref.shape[0]

    loads = []
    for i, ref in enumerate((k_ref, v_ref, q_ref)):
        c = pltpu.make_async_copy(ref, vbuf.at[i], load_sem.at[i])
        c.start()
        loads.append(c)

    barrier = pltpu.get_barrier_semaphore()
    for d in range(1, NY):
        pl.semaphore_signal(barrier, inc=1, device_id={"ctx": z * NY + lax.rem(y + d, NY)}, device_id_type=MESH)
    for d in range(1, nz):
        pl.semaphore_signal(barrier, inc=1, device_id={"ctx": lax.rem(z + d, nz) * NY + y}, device_id_type=MESH)
    pl.semaphore_signal(barrier, inc=1, device_id={"ctx": nxt}, device_id_type=MESH)
    pl.semaphore_signal(barrier, inc=1, device_id={"ctx": prv}, device_id_type=MESH)
    fill = fill_ref[0]
    counts[z, y] = jnp.full((1, LANES), fill, I32)
    pl.semaphore_wait(barrier, NY - 1 + nz - 1 + 2)

    ycopies = []
    for d in range(1, NY):
        c = pltpu.make_async_remote_copy(
            src_ref=counts.at[z, y], dst_ref=counts.at[z, y], send_sem=ysend.at[d], recv_sem=yrecv.at[d],
            device_id={"ctx": z * NY + lax.rem(y + d, NY)}, device_id_type=MESH)
        c.start()
        ycopies.append(c)

    heads = []
    row = 0
    for i, (ref, count) in enumerate(((q_ref, HALO), (g_ref, HALO), (k_ref, NEAR), (v_ref, NEAR))):
        c = pltpu.make_async_remote_copy(
            src_ref=ref.at[pl.ds(0, count)], dst_ref=from_next.at[pl.ds(row, count)],
            send_sem=hsend.at[i], recv_sem=hrecv.at[i], device_id={"ctx": prv}, device_id_type=MESH)
        c.start()
        heads.append(c)
        row += count

    row = 0
    for i, count in enumerate((HALO, HALO, NEAR)):
        loads[i].wait()
        at = lax.broadcasted_iota(I32, (count, rows), 0) + (fill - count)
        pick = (at == lax.broadcasted_iota(I32, (count, rows), 1)).astype(BF16)
        tails[row:row + count, :] = jnp.dot(pick, vbuf[i], preferred_element_type=F32).astype(BF16)
        c = pltpu.make_async_remote_copy(
            src_ref=tails.at[pl.ds(row, count)], dst_ref=from_prev.at[pl.ds(row, count)],
            send_sem=hsend.at[4 + i], recv_sem=hrecv.at[4 + i], device_id={"ctx": nxt}, device_id_type=MESH)
        c.start()
        heads.append(c)
        row += count

    for c in ycopies:
        c.wait()
    zcopies = []
    for d in range(1, nz):
        c = pltpu.make_async_remote_copy(
            src_ref=counts.at[z], dst_ref=counts.at[z], send_sem=zsend.at[d], recv_sem=zrecv.at[d],
            device_id={"ctx": lax.rem(z + d, nz) * NY + y}, device_id_type=MESH)
        c.start()
        zcopies.append(c)
    for c in zcopies:
        c.wait()
    shard = (lax.broadcasted_iota(I32, counts.shape, 0) * NY + lax.broadcasted_iota(I32, counts.shape, 1))
    first_ref[...] = jnp.sum(jnp.where(shard < me, counts[...], 0), axis=(0, 1))
    for c in heads:
        c.wait()


def halo_call(nz, fill, q, k, v, g):
    rows, ch = q.shape
    return pl.pallas_call(
        lambda *refs: halo_kernel(nz, *refs),
        out_shape=(
            jax.ShapeDtypeStruct((1, LANES), I32),
            jax.ShapeDtypeStruct((2 * HALO + NEAR, ch), BF16),
            jax.ShapeDtypeStruct((2 * HALO + 2 * NEAR, ch), BF16),
        ),
        in_specs=[pl.BlockSpec(memory_space=pltpu.SMEM)] + [pl.BlockSpec(memory_space=pl.ANY)] * 4,
        out_specs=(
            pl.BlockSpec(memory_space=pltpu.VMEM),
            pl.BlockSpec(memory_space=pl.ANY),
            pl.BlockSpec(memory_space=pl.ANY),
        ),
        scratch_shapes=[
            pltpu.VMEM((3, rows, ch), BF16),
            pltpu.VMEM((2 * HALO + NEAR, ch), BF16),
            pltpu.VMEM((nz, NY, 1, LANES), I32),
            pltpu.SemaphoreType.DMA((3,)),
            pltpu.SemaphoreType.DMA((NY,)),
            pltpu.SemaphoreType.DMA((NY,)),
            pltpu.SemaphoreType.DMA((nz,)),
            pltpu.SemaphoreType.DMA((nz,)),
            pltpu.SemaphoreType.DMA((7,)),
            pltpu.SemaphoreType.DMA((7,)),
        ],
        compiler_params=pltpu.CompilerParams(collective_id=0, has_side_effects=True, vmem_limit_bytes=60 << 20),
        name="halo",
    )(fill, q, k, v, g)


OFF = HALO
QOFF = NEAR
OUT = 272
WIN = 400
MSLOT = 128


def mix_kernel(n, first_ref, fill_ref, docs_ref, q_ref, k_ref, v_ref, g_ref, hn_ref, hp_ref, ft_ref, taps_ref, skip_ref,
               ho_ref, qg_ref, kg_ref, vg_ref, pk_ref,
               qx, kx, vx, gw, query, keys, values, qb, kb, vb, m, gx, mown, dist, near, maskf, maskb, maskp, shift, taps):
    step = pl.program_id(0)
    rows = q_ref.shape[0]
    fill = fill_ref[0]
    last = lax.axis_index("ctx") == n - 1

    @pl.when(step == 0)
    def _():
        first = first_ref[0, 0]
        begins = [docs_ref[i] - first for i in range(docs_ref.shape[0])]
        end = jnp.where(last, fill, BIG)

        def doc_begin(slot):
            found = jnp.full(slot.shape, -BIG, I32)
            for b in begins:
                found = jnp.where(slot >= b, jnp.maximum(found, b), found)
            return found

        slot = lax.broadcasted_iota(I32, dist.shape, 0) - MSLOT
        dist[...] = slot - doc_begin(slot)
        slot = lax.broadcasted_iota(I32, near.shape, 0)
        until = jnp.full(slot.shape, BIG, I32)
        for b in begins:
            until = jnp.where(slot < b, jnp.minimum(until, b), until)
        near[...] = jnp.where(slot < fill, jnp.minimum(until, end) - 1 - slot, -1)
        for b, count in ((0, 128), (1, 128), (2, 16)):
            shape = (count, 256)
            a = lax.broadcasted_iota(I32, shape, 0)
            lane = lax.broadcasted_iota(I32, shape, 1)
            p, source = 128 * b + a, 128 * (b - 1) + lane
            j = p - source
            keep = (j >= 0) & (j < FILT) & (source >= doc_begin(p))
            maskf[128 * b:128 * b + count, :] = keep.astype(F32).astype(BF16)
            later = 128 * b + lane
            j = later - p
            begin = jnp.where(later < end, doc_begin(later), BIG)
            keep = (j >= 0) & (j < FILT) & (p >= begin)
            maskb[128 * b:128 * b + count, :] = keep.astype(F32).astype(BF16)
            if b < 2:
                p = 128 * b + 127 - a
                j = later - p
                maskp[128 * b:128 * b + count, :] = ((j >= 0) & (j < FILT) & (p >= begin)).astype(F32)
        r = lax.broadcasted_iota(I32, shift.shape, 0) + 192
        shift[...] = (r - fill == lax.broadcasted_iota(I32, shift.shape, 1)).astype(F32).astype(BF16)
        m[MSLOT + OUT:, :] = jnp.zeros((m.shape[0] - MSLOT - OUT, LANES), BF16)
        gx[WIN:, :] = jnp.zeros((gx.shape[0] - WIN, LANES), BF16)
        taps[...] = taps_ref[...].astype(F32)

    def own_or_next(ref, moved, begin, count):
        slot = lax.broadcasted_iota(I32, (count, LANES), 0) + begin
        return jnp.where(slot < fill, ref[begin:begin + count, :].astype(F32), moved)

    kx[0:OFF, :] = hn_ref[0:HALO, :].astype(F32)
    vx[0:OFF, :] = hn_ref[HALO:2 * HALO, :].astype(F32)
    qx[0:QOFF, :] = hn_ref[2 * HALO:2 * HALO + NEAR, :].astype(F32)
    moved_q = jnp.dot(shift[...], hp_ref[0:HALO, :], preferred_element_type=F32)
    moved_g = jnp.dot(shift[...], hp_ref[HALO:2 * HALO, :], preferred_element_type=F32)
    moved_k = jnp.dot(shift[0:80, 0:NEAR], hp_ref[2 * HALO:2 * HALO + NEAR, :], preferred_element_type=F32)
    moved_v = jnp.dot(shift[0:80, 0:NEAR], hp_ref[2 * HALO + NEAR:2 * HALO + 2 * NEAR, :], preferred_element_type=F32)
    for ref, out, off, moved in ((q_ref, qx, QOFF, moved_q), (g_ref, gw, 0, moved_g), (k_ref, kx, OFF, moved_k), (v_ref, vx, OFF, moved_v)):
        out[off:off + 192, :] = ref[0:192, :].astype(F32)
        out[off + 192:off + 256, :] = own_or_next(ref, moved[0:64], 192, 64)
        out[off + 256:off + 192 + moved.shape[0], :] = moved[64:]

    feat = [ft_ref[w].astype(F32) for w in range(3)]
    block = 16

    def featurize(window, at, far, w):
        acc = feat[w][0:1, :] * window[at:at + block, :]
        for j in range(1, SHORT):
            acc = acc + jnp.where(far >= j, feat[w][j:j + 1, :] * window[at - j:at - j + block, :], 0.0)
        return acc

    for s in range(-MSLOT, OUT, block):
        far = dist[s + MSLOT:s + MSLOT + block, :]
        key_rows = featurize(kx, OFF + s, far, 1)
        value_rows = featurize(vx, OFF + s, far, 2)
        m[MSLOT + s:MSLOT + s + block, :] = (key_rows * value_rows).astype(BF16)
        if s >= 0:
            keys[s:s + block, :] = key_rows
            values[s:s + block, :] = value_rows
    for s in range(0, WIN, block):
        far = dist[s + MSLOT:s + MSLOT + block, :]
        query_rows = featurize(qx, QOFF + s, far, 0)
        gx[s:s + block, :] = (query_rows * gw[s:s + block, :]).astype(BF16)
        if s < rows:
            query[s:s + block, :] = query_rows

    flip = (lax.broadcasted_iota(I32, (128, 128), 0) + lax.broadcasted_iota(I32, (128, 128), 1)) == 127
    for at in range(0, rows, 128):
        inside = lax.broadcasted_iota(I32, (128, 128), 1) + at < fill
        pick = jnp.where(flip & inside, 1.0, 0.0).astype(BF16)
        mown[at:at + 128, :] = jnp.dot(pick, m[MSLOT + at:MSLOT + at + 128, :], preferred_element_type=F32).astype(BF16)

    group_of = lax.broadcasted_iota(I32, (128, LANES), 1) // GROUP
    my_taps = taps[pl.ds(pl.multiple_of(step * 8, 8), 8), :]
    reverse = (lax.broadcasted_iota(I32, (FILT, FILT), 0) + lax.broadcasted_iota(I32, (FILT, FILT), 1)) % FILT == 0
    turned = jnp.dot(my_taps.astype(BF16), reverse.astype(F32).astype(BF16), preferred_element_type=F32)

    def circulant(row):
        return pltpu.roll(jnp.broadcast_to(row, (FILT, FILT)), 0, 1, stride=1, stride_axis=0)

    blocks = ((0, 128), (1, 128), (2, 16))
    skip = skip_ref[...]

    acc = [jnp.zeros((count, LANES), F32) for _, count in blocks]
    for g in range(8):
        circ = circulant(turned[g:g + 1, :]).astype(BF16)
        for b, count in blocks:
            both = jnp.concatenate([circ[:count], circ[:count]], axis=1) * maskf[128 * b:128 * b + count, :]
            res = jnp.dot(both, m[128 * b:128 * b + 256, :], preferred_element_type=F32)
            acc[b] = jnp.where(group_of[:count] == g, res, acc[b])
    for b, count in blocks:
        at = 128 * b
        gated = acc[b] + skip * m[MSLOT + at:MSLOT + at + count, :].astype(F32)
        qb[at:at + count, :] = (gw[at:at + count, :] * gated).astype(BF16).astype(F32)
        if b < 2:
            inside = lax.broadcasted_iota(I32, (count, LANES), 0) + at < fill
            ho_ref[at:at + count, :] = jnp.where(inside, query[at:at + count, :] * gated, 0.0).astype(BF16)

    acc = [jnp.zeros((count, LANES), F32) for _, count in blocks]
    mix_rows = []
    for g in range(8):
        circ = circulant(my_taps[g:g + 1, :]).astype(BF16)
        fold = jnp.zeros((128, FILT), F32)
        for b, count in blocks:
            both = jnp.concatenate([circ[:count], circ[:count]], axis=1) * maskb[128 * b:128 * b + count, :]
            window = gx[128 * b:128 * b + 256, :]
            res = jnp.dot(both, window, preferred_element_type=F32)
            acc[b] = jnp.where(group_of[:count] == g, res, acc[b])
            if b < 2:
                mine = jnp.where(group_of == g, mown[128 * b:128 * b + 128, :], jnp.zeros((), BF16))
                prod = lax.dot_general(mine, window, (((1,), (1,)), ((), ())), preferred_element_type=F32)
                prod = prod * maskp[128 * b:128 * b + 128, :]
                fold = fold + prod[:, :128] + prod[:, 128:]
        turned_back = pltpu.roll(fold, 1, 1, stride=1, stride_axis=0)
        mix_rows.append(jnp.sum(turned_back, axis=0, keepdims=True))
    for b, count in blocks:
        at = 128 * b
        back = acc[b] + skip * gx[at:at + count, :].astype(F32)
        kb[at:at + count, :] = (back * values[at:at + count, :]).astype(BF16).astype(F32)
        vb[at:at + count, :] = (back * keys[at:at + count, :]).astype(BF16).astype(F32)

    slot = lax.broadcasted_iota(I32, (rows, LANES), 0)
    both = m[MSLOT:MSLOT + rows, :].astype(F32) * gx[0:rows, :].astype(F32)
    skip_row = jnp.sum(jnp.where(slot < fill, both, 0.0), axis=0, keepdims=True)
    feat_rows = []
    for w, (back, window, off, out) in enumerate(((qb, qx, QOFF, qg_ref), (kb, kx, OFF, kg_ref), (vb, vx, OFF, vg_ref))):
        sums = [jnp.zeros((block, LANES), F32) for _ in range(SHORT)]
        for s in range(0, rows, block):
            reach = near[s:s + block, :]
            source = window[off + s:off + s + block, :]
            total = jnp.zeros((block, LANES), F32)
            for j in range(SHORT):
                later = jnp.where(reach >= j, back[s + j:s + j + block, :], 0.0)
                total = total + feat[w][j:j + 1, :] * later
                sums[j] = sums[j] + source * later
            out[s:s + block, :] = total.astype(BF16)
        feat_rows += [jnp.sum(x, axis=0, keepdims=True) for x in sums]
    packed = jnp.concatenate(mix_rows + [skip_row] + feat_rows + [jnp.zeros((2, LANES), F32)], axis=0)
    for i in range(8):
        pk_ref[i] = packed[4 * i:4 * i + 4, :]


def mix_call(n, first, fill, docs, q, k, v, g, hn, hp, ft, taps, skip):
    rows, ch = q.shape
    steps = ch // LANES
    col = lambda count: pl.BlockSpec((count, LANES), lambda i: (0, i))
    smem = pl.BlockSpec(memory_space=pltpu.SMEM)
    return pl.pallas_call(
        lambda *refs: mix_kernel(n, *refs),
        grid=(steps,),
        out_shape=tuple(jax.ShapeDtypeStruct((rows, ch), BF16) for _ in range(4))
        + (jax.ShapeDtypeStruct((8 * steps, 4, LANES), F32),),
        in_specs=[smem, smem, smem, col(rows), col(rows), col(rows), col(rows), col(hn.shape[0]), col(hp.shape[0]),
                  pl.BlockSpec((3, SHORT, LANES), lambda i: (0, 0, i)), pl.BlockSpec(taps.shape, lambda i: (0, 0)), col(1)],
        out_specs=(col(rows), col(rows), col(rows), col(rows), pl.BlockSpec((8, 4, LANES), lambda i: (i, 0, 0))),
        scratch_shapes=[
            pltpu.VMEM((QOFF + WIN, LANES), F32),
            pltpu.VMEM((OFF + OUT, LANES), F32),
            pltpu.VMEM((OFF + OUT, LANES), F32),
            pltpu.VMEM((WIN, LANES), F32),
            pltpu.VMEM((rows, LANES), F32),
            pltpu.VMEM((OUT, LANES), F32),
            pltpu.VMEM((OUT, LANES), F32),
            pltpu.VMEM((OUT, LANES), F32),
            pltpu.VMEM((OUT, LANES), F32),
            pltpu.VMEM((OUT, LANES), F32),
            pltpu.VMEM((512, LANES), BF16),
            pltpu.VMEM((512, LANES), BF16),
            pltpu.VMEM((rows, LANES), BF16),
            pltpu.VMEM((MSLOT + WIN, LANES), I32),
            pltpu.VMEM((rows, LANES), I32),
            pltpu.VMEM((OUT, 256), BF16),
            pltpu.VMEM((OUT, 256), BF16),
            pltpu.VMEM((rows, 256), F32),
            pltpu.VMEM((WIN - 192, HALO), BF16),
            pltpu.VMEM(taps.shape, F32),
        ],
        compiler_params=pltpu.CompilerParams(vmem_limit_bytes=60 << 20),
        name="mix",
    )(first, fill, docs, q, k, v, g, hn, hp, ft, taps, skip)


def sum_kernel(nz, ntp, params, pk_ref, mix_ref, skip_ref, feat_ref,
               got_y, part, got_z, full, squares, s1, r1, s2, r2, s3, r3, s4, r4, s5, r5):
    me = lax.axis_index("ctx")
    tp = lax.axis_index("tp")
    z, y = me // NY, me % NY

    def across_y(d):
        return {"ctx": z * NY + lax.rem(y + d, NY)}

    def across_z(d):
        return {"ctx": lax.rem(z + d, nz) * NY + y}

    def plane(e):
        dy, dt = e // ntp, e % ntp
        return {"ctx": z * NY + lax.rem(y + dy, NY), "tp": lax.rem(tp + dt, ntp)}

    barrier = pltpu.get_barrier_semaphore()
    for d in range(1, nz):
        pl.semaphore_signal(barrier, inc=1, device_id=across_z(d), device_id_type=MESH)
    for e in range(1, NY * ntp):
        pl.semaphore_signal(barrier, inc=1, device_id=plane(e), device_id_type=MESH)
    pl.semaphore_wait(barrier, nz - 1 + NY * ntp - 1)

    def send(src, dst, ssem, rsem, device):
        c = pltpu.make_async_remote_copy(src_ref=src, dst_ref=dst, send_sem=ssem, recv_sem=rsem,
                                         device_id=device, device_id_type=MESH)
        c.start()
        return c

    copies = [send(pk_ref.at[pl.ds(lax.rem(y + d, NY) * nz, nz)], got_y.at[d], s1.at[d], r1.at[d], across_y(d))
              for d in range(1, NY)]
    for c in copies:
        c.wait()
    total = pk_ref[pl.ds(y * nz, nz)]
    for d in range(1, NY):
        total = total + got_y[d]
    part[...] = total
    copies = [send(part.at[lax.rem(z + d, nz)], got_z.at[d], s2.at[d], r2.at[d], across_z(d)) for d in range(1, nz)]
    for c in copies:
        c.wait()
    piece = part[z]
    for d in range(1, nz):
        piece = piece + got_z[d]
    full[y * nz + z] = piece
    copies = [send(full.at[y * nz + z], full.at[y * nz + z], s3.at[d], r3.at[d], across_z(d)) for d in range(1, nz)]
    for c in copies:
        c.wait()
    mine = pl.ds(y * nz, nz)
    copies = [send(full.at[mine], full.at[mine], s4.at[d], r4.at[d], across_y(d)) for d in range(1, NY)]
    own = full[mine]
    square = jnp.sum(jnp.sum(own * own, axis=0), axis=0, keepdims=True)
    squares[y, tp] = jnp.broadcast_to(jnp.sum(square, axis=1, keepdims=True), (1, LANES))
    copies += [send(squares.at[y, tp], squares.at[y, tp], s5.at[e], r5.at[e], plane(e)) for e in range(1, NY * ntp)]
    for c in copies:
        c.wait()
    whole = jnp.sum(squares[...], axis=(0, 1))
    factor = lax.rsqrt(whole / params + 1e-06)
    for k in range(full.shape[0] // 8):
        mix_ref[8 * k:8 * k + 4, :] = full[8 * k] * factor
        mix_ref[8 * k + 4:8 * k + 8, :] = full[8 * k + 1] * factor
        lanes = slice(LANES * k, LANES * k + LANES)
        skip_ref[:, lanes] = full[8 * k + 2, 0:1] * factor
        for i in range(3 * SHORT):
            r = 9 + i
            feat_ref[i // SHORT, i % SHORT:i % SHORT + 1, lanes] = full[8 * k + r // 4, r % 4:r % 4 + 1] * factor


def sum_call(nz, ntp, params, pk, groups, ch):
    vmem = pl.BlockSpec(memory_space=pltpu.VMEM)
    dma = pltpu.SemaphoreType.DMA
    return pl.pallas_call(
        lambda *refs: sum_kernel(nz, ntp, params, *refs),
        out_shape=(
            jax.ShapeDtypeStruct((groups, FILT), F32),
            jax.ShapeDtypeStruct((1, ch), F32),
            jax.ShapeDtypeStruct((3, SHORT, ch), F32),
        ),
        in_specs=[vmem],
        out_specs=(vmem, vmem, vmem),
        scratch_shapes=[
            pltpu.VMEM((NY, nz, 4, LANES), F32),
            pltpu.VMEM((nz, 4, LANES), F32),
            pltpu.VMEM((nz, 4, LANES), F32),
            pltpu.VMEM((NY * nz, 4, LANES), F32),
            pltpu.VMEM((NY, ntp, 1, LANES), F32),
            dma((NY,)), dma((NY,)), dma((nz,)), dma((nz,)), dma((nz,)), dma((nz,)), dma((NY,)), dma((NY,)),
            dma((NY * ntp,)), dma((NY * ntp,)),
        ],
        compiler_params=pltpu.CompilerParams(collective_id=1, has_side_effects=True, vmem_limit_bytes=60 << 20),
        name="total",
    )(pk)


def solution(mesh):
    n, ntp = mesh.shape["ctx"], mesh.shape["tp"]
    nz = n // NY

    def shards(q, k, v, g, fill, docs, ft, taps, skip):
        groups, ch = taps.shape[0], q.shape[1]
        params = (groups * FILT + ch * (1 + 3 * SHORT)) * ntp
        first, hn, hp = halo_call(nz, fill, q, k, v, g)
        ho, qg, kg, vg, pk = mix_call(n, first, fill, docs, q, k, v, g, hn, hp, ft, taps, skip.reshape(1, ch))
        mix_grad, skip_grad, feat_grad = sum_call(nz, ntp, params, pk, groups, ch)
        return ho, qg, kg, vg, mix_grad, skip_grad.reshape(ch), feat_grad

    rows, whole = P("ctx", "tp"), P(None, None, "tp")
    return jax.shard_map(
        shards, mesh=mesh,
        in_specs=(rows, rows, rows, rows, P("ctx"), P(), whole, P("tp", None), P("tp")),
        out_specs=(rows, rows, rows, rows, P("tp", None), P("tp"), whole),
        check_vma=False)
```

time: 874 us -> 98.4 us (0.11)
  waiting for transfers between devices: 301 us -> 0 us
  blocking collectives: 273 us -> 0 us
  local copies, waits for them, and re-layouts: 141 us -> 3.51 us
  Pallas kernels: 0 us -> 93.3 us
  other arithmetic: 49.1 us -> 0 us
  loops' own time: 45.7 us -> 0 us
  matrix products: 24.5 us -> 0 us
  starting transfers between devices: 17.8 us -> 0 us
  between operations: 18.5 us -> 1.31 us
    psum x1 -> x0, waiting for transfers between devices: 301 us -> none  [shards(): taps_sum, skip_sum, feat_sum = lax.psum((taps_grad, skip_part, feat), 'ctx')]
    psum x2 -> x0, blocking collectives: 246 us -> none  [the longest x1 223 us: shards(): taps_sum, skip_sum, feat_sum = lax.psum((taps_grad, skip_part, feat), 'ctx')]
    pallas_call x0 -> x3, Pallas kernels: none -> 93.3 us  [the longest x1 38.3 us: sum_call(): pl.pallas_call(lambda *refs: sum_kernel(nz, ntp, params, *refs), out_shap...]
    reshape x4 -> x0, local copies, waits for them, and re-layouts: 50.2 us -> none  [the longest x2 31.7 us: banded(): tiled[:, :block_rows * window].reshape(group_count, block_rows, window)]
    dynamic_slice x89 -> x0, local copies, waits for them, and re-layouts: 46.8 us -> none  [the longest x63 36.8 us: turn(): longer = join(so_far, pieces[position])]
    another operation x3 -> x0, loops' own time: 45.7 us -> none  [the longest x1 42.9 us: prefix(): return lax.fori_loop(0, count - 1, turn, so_far)]
    reduce_sum x15 -> x0, other arithmetic: 35.2 us -> none  [the longest x6 15.7 us: feat_grads(): jnp.sum(jnp.where(same_doc, source * grads.astype(jnp.float32), 0.0), axi...]
    unnamed x1 -> x0, blocking collectives: 26.5 us -> none
  transfers between devices with their start and end apart: 9 -> 0, of which waited for: 1 -> 0; matrix products, arithmetic and copies ran while one was open for 22% -> 0% of each run, Pallas kernels for 0% -> 0%
where the time goes in v1:
time: 98.4 us; the launch traced here: 98.1 us
  Pallas kernels  93.3 us (95%)
  local copies, waits for them, and re-layouts  3.51 us (4%)
  between operations  1.31 us (1%)
    pallas_call x1, Pallas kernels, sum_call(): pl.pallas_call(lambda *refs: sum_kernel(nz, ntp, params, *refs), out_shap...  38.3 us
    pallas_call x1, Pallas kernels, halo_call(): pl.pallas_call(lambda *refs: halo_kernel(nz, *refs), out_shape=(jax.Shape...  34 us
    pallas_call x1, Pallas kernels, mix_call(): pl.pallas_call(lambda *refs: mix_kernel(n, *refs), grid=(steps,), out_sha...  21 us
    unnamed x5, local copies, waits for them, and re-layouts  3.51 us

profile of v1, /device:TPU:1, one launch (start us, length us, event | category | flops | bytes accessed | tf_op | source)
XLA Modules:
  0.0 98.1 jit_solution(17643680952834898024)
XLA Ops:
  1.3 34.0 %halo.1 = (s32[1,128]{1,0:T(1,128)}, bf16[304,1024]{1,0:T(8,128)(2,1)}, bf16[320,1024]{1,0:T(8,128)(2,1)}) custom-call(s32[1]{0:T(128)S(6)} %copy.19.refs_0_.refs_1_, bf16[256,1024]{1,0:T(8,128)(2,1)} %refs_3_.3, bf16[256,1024]{1,0:T(8,128)(2,1)} %refs_4_.3, bf16[256,1024]{1,0:T(8,128)(2,1)} %refs_5_.1, bf16[256,1024]{1,0:T(8,128)(2,1)} %refs_6_.1), custom_call_target="tpu_custom_call" | custom-call | tf_op jit(solution)/shard_map/halo/pallas_call | solution.py:98
  35.3 21.0 %mix.1 = (bf16[256,1024]{1,0:T(8,128)(2,1)}, bf16[256,1024]{1,0:T(8,128)(2,1)}, bf16[256,1024]{1,0:T(8,128)(2,1)}, bf16[256,1024]{1,0:T(8,128)(2,1)}, f32[64,4,128]{2,1,0:T(4,128)}) custom-call(s32[1,128]{1,0:T(1,128)} %get-tuple-element.18.refs_0_, s32[1]{0:T(128)S(6)} %copy.19.refs_0_.refs_1_, s32[4]{0:T(128)} %refs_2_.3, bf16[256,1024]{1,0:T(8,128)(2,1)} %refs_3_.3, ...), custom_call_target="tpu_custom_call" | custom-call | tf_op jit(solution)/shard_map/mix/pallas_call | solution.py:306
  56.3 38.3 %total.1 = (f32[64,128]{1,0:T(8,128)}, f32[1,1024]{1,0:T(1,128)}, f32[3,7,1024]{2,1,0:T(8,128)}) custom-call(f32[64,4,128]{2,1,0:T(4,128)} %get-tuple-element.25.refs_0_), custom_call_target="tpu_custom_call" | custom-call | tf_op jit(solution)/shard_map/total/pallas_call | solution.py:411
  94.6 0.0 copy-start
  94.6 1.4 %copy.20 = f32[64,128]{1,0:T(8,128)} copy(f32[64,128]{1,0:T(8,128)} %get-tuple-element.40) | data formatting | bytes 65536
  96.0 0.0 copy-done
  96.0 0.6 copy.21
  96.6 1.5 %copy.22 = f32[3,7,1024]{2,1,0:T(8,128)} copy(f32[3,7,1024]{2,1,0:T(8,128)} %get-tuple-element.42) | data formatting | bytes 172032
Async XLA Ops:
  94.6 1.4 %copy-start = (f32[1,1024]{1,0:T(1,128)S(1)}, f32[1,1024]{1,0:T(1,128)}, u32[]{:S(2)}) copy-start(f32[1,1024]{1,0:T(1,128)} %get-tuple-element.27) | copy-start | bytes 12292

commit v2 on v1

v2 whole, which is shorter than its diff:
```python
import jax
import jax.numpy as jnp
from jax import lax
from jax.experimental import pallas as pl
from jax.experimental.pallas import tpu as pltpu
from jax.sharding import PartitionSpec as P

F32 = jnp.float32
BF16 = jnp.bfloat16
I32 = jnp.int32
MESH = pl.DeviceIdType.MESH

NY = 4
HALO = 144
NEAR = 16
LANES = 128
SHORT = 7
FILT = 128
GROUP = 16
BIG = 1 << 28

OFF = HALO
QOFF = NEAR
OUT = 272
WIN = 400
MSLOT = 128

NEAREST = 16
NZB = 4


def mesh_copy(src, dst, ssem, rsem, device):
    c = pltpu.make_async_remote_copy(src_ref=src, dst_ref=dst, send_sem=ssem, recv_sem=rsem,
                                     device_id=device, device_id_type=MESH)
    c.start()
    return c


class Peers:
    def __init__(self, nz, ntp):
        self.nz, self.ntp = nz, ntp
        self.me = lax.axis_index("ctx")
        self.tp = lax.axis_index("tp")
        self.z, self.y = self.me // NY, self.me % NY
        self.za, self.zb = self.z // NZB, self.z % NZB
        self.nza = nz // NZB

    def along_y(self, d):
        return {"ctx": self.z * NY + lax.rem(self.y + d, NY)}

    def along_z(self, d):
        return {"ctx": lax.rem(self.z + d, self.nz) * NY + self.y}

    def step(self, d):
        return {"ctx": lax.rem(self.me + d + self.nz * NY, self.nz * NY)}

    def near(self, e):
        y, zb = lax.rem(self.y + e // NZB, NY), lax.rem(self.zb + e % NZB, NZB)
        return y * NZB + zb, {"ctx": (self.za * NZB + zb) * NY + y}

    def far(self, d):
        return {"ctx": (lax.rem(self.za + d, self.nza) * NZB + self.zb) * NY + self.y}

    def along_tp(self, d):
        return {"tp": lax.rem(self.tp + d, self.ntp)}


def exchange(at, fill, q_ref, k_ref, v_ref, g_ref, first, hn, hp, vbuf, tails, counts,
             load_sem, ysend, yrecv, zsend, zrecv, hsend, hrecv):
    nz, rows = at.nz, q_ref.shape[0]
    loads = []
    for i, ref in enumerate((k_ref, v_ref, q_ref)):
        c = pltpu.make_async_copy(ref, vbuf.at[i], load_sem.at[i])
        c.start()
        loads.append(c)

    barrier = pltpu.get_barrier_semaphore()
    partners = [at.along_y(d) for d in range(1, NY)] + [at.along_z(d) for d in range(1, nz)] + [at.step(1), at.step(-1)]
    partners += [at.near(e)[1] for e in range(1, NEAREST)] + [at.along_tp(d) for d in range(1, at.ntp)]
    for device in partners:
        pl.semaphore_signal(barrier, inc=1, device_id=device, device_id_type=MESH)
    counts[at.z, at.y] = jnp.full((1, LANES), fill, I32)
    pl.semaphore_wait(barrier, len(partners))

    own = counts.at[at.z, at.y]
    ycopies = [mesh_copy(own, own, ysend.at[d], yrecv.at[d], at.along_y(d)) for d in range(1, NY)]
    copies = []
    row = 0
    for i, (ref, count) in enumerate(((q_ref, HALO), (g_ref, HALO), (k_ref, NEAR), (v_ref, NEAR))):
        copies.append(mesh_copy(ref.at[pl.ds(0, count)], hp.at[pl.ds(row, count)], hsend.at[i], hrecv.at[i], at.step(-1)))
        row += count
    row = 0
    for i, count in enumerate((HALO, HALO, NEAR)):
        loads[i].wait()
        slot = lax.broadcasted_iota(I32, (count, rows), 0) + (fill - count)
        pick = (slot == lax.broadcasted_iota(I32, (count, rows), 1)).astype(F32).astype(BF16)
        tails[row:row + count, :] = jnp.dot(pick, vbuf[i], preferred_element_type=F32).astype(BF16)
        part = pl.ds(row, count)
        copies.append(mesh_copy(tails.at[part], hn.at[part], hsend.at[4 + i], hrecv.at[4 + i], at.step(1)))
        row += count
    for c in ycopies:
        c.wait()
    own = counts.at[at.z]
    zcopies = [mesh_copy(own, own, zsend.at[d], zrecv.at[d], at.along_z(d)) for d in range(1, nz)]
    for c in zcopies:
        c.wait()
    shard = lax.broadcasted_iota(I32, counts.shape, 0) * NY + lax.broadcasted_iota(I32, counts.shape, 1)
    first[...] = jnp.sum(jnp.where(shard < at.me, counts[...], 0), axis=(0, 1))
    for c in copies:
        c.wait()


def sum_shards(at, params, raw, got, parts, full, squares, s1, r1, s2, r2, s3, r3, s4, r4, out_ref):
    mine = at.y * NZB + at.zb
    copies = []
    for e in range(1, NEAREST):
        piece, device = at.near(e)
        copies.append(mesh_copy(raw.at[piece], got.at[e], s1.at[e], r1.at[e], device))
    for c in copies:
        c.wait()
    acc = raw[mine]
    for e in range(1, NEAREST):
        acc = acc + got[e]
    parts[at.za] = acc
    own = parts.at[at.za]
    copies = [mesh_copy(own, own, s2.at[d], r2.at[d], at.far(d)) for d in range(1, at.nza)]
    for c in copies:
        c.wait()
    acc = parts[0]
    for d in range(1, at.nza):
        acc = acc + parts[d]
    full[mine] = acc
    own = full.at[mine]
    copies = [mesh_copy(own, own, s3.at[e], r3.at[e], at.near(e)[1]) for e in range(1, NEAREST)]
    for c in copies:
        c.wait()
    square = jnp.zeros(full.shape[1:], F32)
    for i in range(NEAREST):
        square = square + full[i] * full[i]
    square = jnp.sum(jnp.sum(square, axis=0, keepdims=True), axis=1, keepdims=True)
    squares[at.tp] = jnp.broadcast_to(square, (1, LANES))
    own = squares.at[at.tp]
    copies = [mesh_copy(own, own, s4.at[d], r4.at[d], at.along_tp(d)) for d in range(1, at.ntp)]
    for c in copies:
        c.wait()
    factor = lax.rsqrt(jnp.sum(squares[...], axis=0) / params + 1e-06)
    for i in range(NEAREST):
        out_ref[i] = full[i] * factor


def mix_kernel(nz, ntp, params, fill_ref, docs_ref, qw_ref, kw_ref, vw_ref, gw_ref, q_ref, k_ref, v_ref, g_ref, ft_ref, taps_ref, skip_ref,
               ho_ref, qg_ref, kg_ref, vg_ref, pk_ref,
               qx, kx, vx, gw, query, keys, values, qb, kb, vb, m, gx, mown, dist, near, maskf, maskb, maskp, shift, taps,
               first_row, hn, hp, vbuf, tails, counts, raw, got, parts, full, squares,
               load_sem, ysend, yrecv, zsend, zrecv, hsend, hrecv, s1, r1, s2, r2, s3, r3, s4, r4):
    step = pl.program_id(0)
    rows = q_ref.shape[0]
    fill = fill_ref[0]
    peers = Peers(nz, ntp)
    last = peers.me == nz * NY - 1

    @pl.when(step == 0)
    def _():
        exchange(peers, fill, qw_ref, kw_ref, vw_ref, gw_ref, first_row, hn, hp, vbuf, tails, counts,
                 load_sem, ysend, yrecv, zsend, zrecv, hsend, hrecv)
        begin_rows = [docs_ref[i] - first_row[...] for i in range(docs_ref.shape[0])]
        end = jnp.where(last, fill, BIG)

        def doc_begin(slot):
            found = jnp.full(slot.shape, -BIG, I32)
            for b in begin_rows:
                b = jnp.broadcast_to(b[:, 0:1], slot.shape)
                found = jnp.where(slot >= b, jnp.maximum(found, b), found)
            return found

        slot = lax.broadcasted_iota(I32, dist.shape, 0) - MSLOT
        dist[...] = slot - doc_begin(slot)
        slot = lax.broadcasted_iota(I32, near.shape, 0)
        until = jnp.full(slot.shape, BIG, I32)
        for b in begin_rows:
            b = jnp.broadcast_to(b[:, 0:1], slot.shape)
            until = jnp.where(slot < b, jnp.minimum(until, b), until)
        near[...] = jnp.where(slot < fill, jnp.minimum(until, end) - 1 - slot, -1)
        for b, count in ((0, 128), (1, 128), (2, 16)):
            shape = (count, 256)
            a = lax.broadcasted_iota(I32, shape, 0)
            lane = lax.broadcasted_iota(I32, shape, 1)
            p, source = 128 * b + a, 128 * (b - 1) + lane
            j = p - source
            keep = (j >= 0) & (j < FILT) & (source >= doc_begin(p))
            maskf[128 * b:128 * b + count, :] = keep.astype(F32).astype(BF16)
            later = 128 * b + lane
            j = later - p
            begin = jnp.where(later < end, doc_begin(later), BIG)
            keep = (j >= 0) & (j < FILT) & (p >= begin)
            maskb[128 * b:128 * b + count, :] = keep.astype(F32).astype(BF16)
            if b < 2:
                p = 128 * b + 127 - a
                j = later - p
                maskp[128 * b:128 * b + count, :] = ((j >= 0) & (j < FILT) & (p >= begin)).astype(F32)
        r = lax.broadcasted_iota(I32, shift.shape, 0) + 192
        shift[...] = (r - fill == lax.broadcasted_iota(I32, shift.shape, 1)).astype(F32).astype(BF16)
        m[MSLOT + OUT:, :] = jnp.zeros((m.shape[0] - MSLOT - OUT, LANES), BF16)
        gx[WIN:, :] = jnp.zeros((gx.shape[0] - WIN, LANES), BF16)
        taps[...] = taps_ref[...].astype(F32)

    def own_or_next(ref, moved, begin, count):
        slot = lax.broadcasted_iota(I32, (count, LANES), 0) + begin
        return jnp.where(slot < fill, ref[begin:begin + count, :].astype(F32), moved)

    lanes = pl.ds(pl.multiple_of(step * LANES, LANES), LANES)
    kx[0:OFF, :] = hn[0:HALO, lanes].astype(F32)
    vx[0:OFF, :] = hn[HALO:2 * HALO, lanes].astype(F32)
    qx[0:QOFF, :] = hn[2 * HALO:2 * HALO + NEAR, lanes].astype(F32)
    moved_q = jnp.dot(shift[...], hp[0:HALO, lanes], preferred_element_type=F32)
    moved_g = jnp.dot(shift[...], hp[HALO:2 * HALO, lanes], preferred_element_type=F32)
    moved_k = jnp.dot(shift[0:80, 0:NEAR], hp[2 * HALO:2 * HALO + NEAR, lanes], preferred_element_type=F32)
    moved_v = jnp.dot(shift[0:80, 0:NEAR], hp[2 * HALO + NEAR:2 * HALO + 2 * NEAR, lanes], preferred_element_type=F32)
    for ref, out, off, moved in ((q_ref, qx, QOFF, moved_q), (g_ref, gw, 0, moved_g), (k_ref, kx, OFF, moved_k), (v_ref, vx, OFF, moved_v)):
        out[off:off + 192, :] = ref[0:192, :].astype(F32)
        out[off + 192:off + 256, :] = own_or_next(ref, moved[0:64], 192, 64)
        out[off + 256:off + 192 + moved.shape[0], :] = moved[64:]

    feat = [ft_ref[w].astype(F32) for w in range(3)]
    block = 16

    def featurize(window, at, far, w):
        acc = feat[w][0:1, :] * window[at:at + block, :]
        for j in range(1, SHORT):
            acc = acc + jnp.where(far >= j, feat[w][j:j + 1, :] * window[at - j:at - j + block, :], 0.0)
        return acc

    for s in range(-MSLOT, OUT, block):
        far = dist[s + MSLOT:s + MSLOT + block, :]
        key_rows = featurize(kx, OFF + s, far, 1)
        value_rows = featurize(vx, OFF + s, far, 2)
        m[MSLOT + s:MSLOT + s + block, :] = (key_rows * value_rows).astype(BF16)
        if s >= 0:
            keys[s:s + block, :] = key_rows
            values[s:s + block, :] = value_rows
    for s in range(0, WIN, block):
        far = dist[s + MSLOT:s + MSLOT + block, :]
        query_rows = featurize(qx, QOFF + s, far, 0)
        gx[s:s + block, :] = (query_rows * gw[s:s + block, :]).astype(BF16)
        if s < rows:
            query[s:s + block, :] = query_rows

    flip = (lax.broadcasted_iota(I32, (128, 128), 0) + lax.broadcasted_iota(I32, (128, 128), 1)) == 127
    for at in range(0, rows, 128):
        inside = lax.broadcasted_iota(I32, (128, 128), 1) + at < fill
        pick = jnp.where(flip & inside, 1.0, 0.0).astype(BF16)
        mown[at:at + 128, :] = jnp.dot(pick, m[MSLOT + at:MSLOT + at + 128, :], preferred_element_type=F32).astype(BF16)

    group_of = lax.broadcasted_iota(I32, (128, LANES), 1) // GROUP
    my_taps = taps[pl.ds(pl.multiple_of(step * 8, 8), 8), :]
    reverse = (lax.broadcasted_iota(I32, (FILT, FILT), 0) + lax.broadcasted_iota(I32, (FILT, FILT), 1)) % FILT == 0
    turned = jnp.dot(my_taps.astype(BF16), reverse.astype(F32).astype(BF16), preferred_element_type=F32)

    def circulant(row):
        return pltpu.roll(jnp.broadcast_to(row, (FILT, FILT)), 0, 1, stride=1, stride_axis=0)

    blocks = ((0, 128), (1, 128), (2, 16))
    skip = skip_ref[...]

    acc = [jnp.zeros((count, LANES), F32) for _, count in blocks]
    for g in range(8):
        circ = circulant(turned[g:g + 1, :]).astype(BF16)
        for b, count in blocks:
            both = jnp.concatenate([circ[:count], circ[:count]], axis=1) * maskf[128 * b:128 * b + count, :]
            res = jnp.dot(both, m[128 * b:128 * b + 256, :], preferred_element_type=F32)
            acc[b] = jnp.where(group_of[:count] == g, res, acc[b])
    for b, count in blocks:
        at = 128 * b
        gated = acc[b] + skip * m[MSLOT + at:MSLOT + at + count, :].astype(F32)
        qb[at:at + count, :] = (gw[at:at + count, :] * gated).astype(BF16).astype(F32)
        if b < 2:
            inside = lax.broadcasted_iota(I32, (count, LANES), 0) + at < fill
            ho_ref[at:at + count, :] = jnp.where(inside, query[at:at + count, :] * gated, 0.0).astype(BF16)

    acc = [jnp.zeros((count, LANES), F32) for _, count in blocks]
    mix_rows = []
    for g in range(8):
        circ = circulant(my_taps[g:g + 1, :]).astype(BF16)
        fold = jnp.zeros((128, FILT), F32)
        for b, count in blocks:
            both = jnp.concatenate([circ[:count], circ[:count]], axis=1) * maskb[128 * b:128 * b + count, :]
            window = gx[128 * b:128 * b + 256, :]
            res = jnp.dot(both, window, preferred_element_type=F32)
            acc[b] = jnp.where(group_of[:count] == g, res, acc[b])
            if b < 2:
                mine = jnp.where(group_of == g, mown[128 * b:128 * b + 128, :], jnp.zeros((), BF16))
                prod = lax.dot_general(mine, window, (((1,), (1,)), ((), ())), preferred_element_type=F32)
                prod = prod * maskp[128 * b:128 * b + 128, :]
                fold = fold + prod[:, :128] + prod[:, 128:]
        turned_back = pltpu.roll(fold, 1, 1, stride=1, stride_axis=0)
        mix_rows.append(jnp.sum(turned_back, axis=0, keepdims=True))
    for b, count in blocks:
        at = 128 * b
        back = acc[b] + skip * gx[at:at + count, :].astype(F32)
        kb[at:at + count, :] = (back * values[at:at + count, :]).astype(BF16).astype(F32)
        vb[at:at + count, :] = (back * keys[at:at + count, :]).astype(BF16).astype(F32)

    slot = lax.broadcasted_iota(I32, (rows, LANES), 0)
    both = m[MSLOT:MSLOT + rows, :].astype(F32) * gx[0:rows, :].astype(F32)
    skip_row = jnp.sum(jnp.where(slot < fill, both, 0.0), axis=0, keepdims=True)
    feat_rows = []
    for w, (back, window, off, out) in enumerate(((qb, qx, QOFF, qg_ref), (kb, kx, OFF, kg_ref), (vb, vx, OFF, vg_ref))):
        sums = [jnp.zeros((block, LANES), F32) for _ in range(SHORT)]
        for s in range(0, rows, block):
            reach = near[s:s + block, :]
            source = window[off + s:off + s + block, :]
            total = jnp.zeros((block, LANES), F32)
            for j in range(SHORT):
                later = jnp.where(reach >= j, back[s + j:s + j + block, :], 0.0)
                total = total + feat[w][j:j + 1, :] * later
                sums[j] = sums[j] + source * later
            out[s:s + block, :] = total.astype(BF16)
        feat_rows += [jnp.sum(x, axis=0, keepdims=True) for x in sums]
    packed = jnp.concatenate(mix_rows + [skip_row] + feat_rows + [jnp.zeros((2, LANES), F32)], axis=0)
    raw[2 * step] = packed[0:16]
    raw[2 * step + 1] = packed[16:32]

    @pl.when(step == pl.num_programs(0) - 1)
    def _():
        sum_shards(peers, params, raw, got, parts, full, squares, s1, r1, s2, r2, s3, r3, s4, r4, pk_ref)


def mix_call(nz, ntp, params, fill, docs, q, k, v, g, ft, taps, skip):
    rows, ch = q.shape
    steps = ch // LANES
    col = lambda count: pl.BlockSpec((count, LANES), lambda i: (0, i))
    smem = pl.BlockSpec(memory_space=pltpu.SMEM)
    hbm = pl.BlockSpec(memory_space=pl.ANY)
    dma = pltpu.SemaphoreType.DMA
    piece = (16, LANES)
    return pl.pallas_call(
        lambda *refs: mix_kernel(nz, ntp, params, *refs),
        grid=(steps,),
        out_shape=tuple(jax.ShapeDtypeStruct((rows, ch), BF16) for _ in range(4))
        + (jax.ShapeDtypeStruct((NEAREST, *piece), F32),),
        in_specs=[smem, smem, hbm, hbm, hbm, hbm, col(rows), col(rows), col(rows), col(rows),
                  pl.BlockSpec((3, SHORT, LANES), lambda i: (0, 0, i)), pl.BlockSpec(taps.shape, lambda i: (0, 0)), col(1)],
        out_specs=(col(rows), col(rows), col(rows), col(rows), pl.BlockSpec((NEAREST, *piece), lambda i: (0, 0, 0))),
        scratch_shapes=[
            pltpu.VMEM((QOFF + WIN, LANES), F32),
            pltpu.VMEM((OFF + OUT, LANES), F32),
            pltpu.VMEM((OFF + OUT, LANES), F32),
            pltpu.VMEM((WIN, LANES), F32),
            pltpu.VMEM((rows, LANES), F32),
            pltpu.VMEM((OUT, LANES), F32),
            pltpu.VMEM((OUT, LANES), F32),
            pltpu.VMEM((OUT, LANES), F32),
            pltpu.VMEM((OUT, LANES), F32),
            pltpu.VMEM((OUT, LANES), F32),
            pltpu.VMEM((512, LANES), BF16),
            pltpu.VMEM((512, LANES), BF16),
            pltpu.VMEM((rows, LANES), BF16),
            pltpu.VMEM((MSLOT + WIN, LANES), I32),
            pltpu.VMEM((rows, LANES), I32),
            pltpu.VMEM((OUT, 256), BF16),
            pltpu.VMEM((OUT, 256), BF16),
            pltpu.VMEM((rows, 256), F32),
            pltpu.VMEM((WIN - 192, HALO), BF16),
            pltpu.VMEM(taps.shape, F32),
            pltpu.VMEM((1, LANES), I32),
            pltpu.VMEM((2 * HALO + NEAR, ch), BF16),
            pltpu.VMEM((2 * HALO + 2 * NEAR, ch), BF16),
            pltpu.VMEM((3, rows, ch), BF16),
            pltpu.VMEM((2 * HALO + NEAR, ch), BF16),
            pltpu.VMEM((nz, NY, 1, LANES), I32),
            pltpu.VMEM((NEAREST, *piece), F32),
            pltpu.VMEM((NEAREST, *piece), F32),
            pltpu.VMEM((nz // NZB, *piece), F32),
            pltpu.VMEM((NEAREST, *piece), F32),
            pltpu.VMEM((ntp, 1, LANES), F32),
            dma((3,)), dma((NY,)), dma((NY,)), dma((nz,)), dma((nz,)), dma((7,)), dma((7,)),
            dma((NEAREST,)), dma((NEAREST,)), dma((nz // NZB,)), dma((nz // NZB,)), dma((NEAREST,)), dma((NEAREST,)),
            dma((ntp,)), dma((ntp,)),
        ],
        compiler_params=pltpu.CompilerParams(collective_id=0, has_side_effects=True, vmem_limit_bytes=60 << 20),
        name="mix",
    )(fill, docs, q, k, v, g, q, k, v, g, ft, taps, skip)


def place_kernel(*refs):
    pk_ref, mix_ref, skip_ref, feat_ref = refs[4], *refs[9:]
    for source, out in zip(refs[:4], refs[5:9]):
        out[...] = source[...]

    @pl.when(pl.program_id(0) == 0)
    def _():
        for k in range(pk_ref.shape[0] // 2):
            lanes = slice(LANES * k, LANES * k + LANES)
            mix_ref[8 * k:8 * k + 8, :] = pk_ref[2 * k, 0:8]
            skip_ref[:, lanes] = pk_ref[2 * k, 8:9]
            for w in range(3):
                for j in range(SHORT):
                    r = 9 + SHORT * w + j
                    feat_ref[w, j:j + 1, lanes] = pk_ref[2 * k + r // 16, r % 16:r % 16 + 1]


def place_call(big, pk, groups):
    rows, ch = big[0].shape
    whole = lambda *shape: pl.BlockSpec(shape, lambda i: (0,) * len(shape))
    part = pl.BlockSpec((64, ch), lambda i: (i, 0))
    return pl.pallas_call(
        place_kernel,
        grid=(rows // 64,),
        out_shape=tuple(jax.ShapeDtypeStruct((rows, ch), BF16) for _ in range(4)) + (
            jax.ShapeDtypeStruct((groups, FILT), F32),
            jax.ShapeDtypeStruct((1, ch), F32),
            jax.ShapeDtypeStruct((3, SHORT, ch), F32),
        ),
        in_specs=[part] * 4 + [whole(*pk.shape)],
        out_specs=(part,) * 4 + (whole(groups, FILT), whole(1, ch), whole(3, SHORT, ch)),
        compiler_params=pltpu.CompilerParams(vmem_limit_bytes=60 << 20),
        name="place",
    )(*big, pk)


def solution(mesh):
    n, ntp = mesh.shape["ctx"], mesh.shape["tp"]
    nz = n // NY

    def shards(q, k, v, g, fill, docs, ft, taps, skip):
        groups, ch = taps.shape[0], q.shape[1]
        params = (groups * FILT + ch * (1 + 3 * SHORT)) * ntp
        *big, pk = mix_call(nz, ntp, params, fill, docs, q, k, v, g, ft, taps, skip.reshape(1, ch))
        *big, mix_grad, skip_grad, feat_grad = place_call(big, pk, groups)
        return *big, mix_grad, skip_grad.reshape(ch), feat_grad

    rows, whole = P("ctx", "tp"), P(None, None, "tp")
    return jax.shard_map(
        shards, mesh=mesh,
        in_specs=(rows, rows, rows, rows, P("ctx"), P(), whole, P("tp", None), P("tp")),
        out_specs=(rows, rows, rows, rows, P("tp", None), P("tp"), whole),
        check_vma=False)
```

time: 98.4 us -> 88.6 us (0.900)
  Pallas kernels: 93.3 us -> 87 us
  local copies, waits for them, and re-layouts: 3.51 us -> 0 us
    pallas_call x3 -> x2, Pallas kernels: 93.3 us -> 87 us  [the longest x1 83 us: mix_call(): pl.pallas_call(lambda *refs: mix_kernel(nz, ntp, params, *refs), grid=(st...]
    unnamed x5 -> x0, local copies, waits for them, and re-layouts: 3.51 us -> none
where the time goes in v2:
time: 88.6 us; the launch traced here: 88.3 us
  Pallas kernels  87 us (98%)
  between operations  1.29 us (1%)
    pallas_call x1, Pallas kernels, mix_call(): pl.pallas_call(lambda *refs: mix_kernel(nz, ntp, params, *refs), grid=(st...  83 us
    pallas_call x1, Pallas kernels, place_call(): pl.pallas_call(place_kernel, grid=(rows // 64,), out_shape=tuple((jax.Sha...  4.03 us

profile of v2, /device:TPU:1, one launch (start us, length us, event | category | flops | bytes accessed | tf_op | source)
XLA Modules:
  0.0 88.3 jit_solution(9651892561111970639)
XLA Ops:
  1.3 83.0 %mix.1 = (bf16[256,1024]{1,0:T(8,128)(2,1)}, bf16[256,1024]{1,0:T(8,128)(2,1)}, bf16[256,1024]{1,0:T(8,128)(2,1)}, bf16[256,1024]{1,0:T(8,128)(2,1)}, f32[16,16,128]{2,1,0:T(8,128)}) custom-call(s32[1]{0:T(128)S(6)} %copy.16.refs_0_, s32[4]{0:T(128)} %refs_1_.1, bf16[256,1024]{1,0:T(8,128)(2,1)} %refs_6_.1, bf16[256,1024]{1,0:T(8,128)(2,1)} %refs_7_.1, ...), custom_call_target="tpu_custom_call" | custom-call | tf_op jit(solution)/shard_map/mix/pallas_call | solution.py:336
  84.3 4.0 %place.1 = (bf16[256,1024]{1,0:T(8,128)(2,1)}, bf16[256,1024]{1,0:T(8,128)(2,1)}, bf16[256,1024]{1,0:T(8,128)(2,1)}, bf16[256,1024]{1,0:T(8,128)(2,1)}, f32[64,1...) custom-call(bf16[256,1024]{1,0:T(8,128)(2,1)} %get-tuple-element.19.refs_0_, ...), custom_call_target="tpu_custom_call" | custom-call | tf_op jit(solution)/shard_map/place/pallas_call | solution.py:406

commit v3 on v2

--- a/solution.py
+++ b/solution.py
@@ -27,6 +27,8 @@
 
 NEAREST = 16
 NZB = 4
+PARTS = ((0, 1), (1, 3), (3, 8))
+TAILS = (HALO, HALO, NEAR)
 
 
 def mesh_copy(src, dst, ssem, rsem, device):
@@ -34,6 +36,11 @@
                                      device_id=device, device_id_type=MESH)
     c.start()
     return c
+
+
+def piece_copy(raw, got, s1, r1, piece, e, device):
+    return pltpu.make_async_remote_copy(src_ref=raw.at[piece], dst_ref=got.at[e], send_sem=s1.at[e], recv_sem=r1.at[e],
+                                        device_id=device, device_id_type=MESH)
 
 
 class Peers:
@@ -61,8 +68,16 @@
     def far(self, d):
         return {"ctx": (lax.rem(self.za + d, self.nza) * NZB + self.zb) * NY + self.y}
 
-    def along_tp(self, d):
-        return {"tp": lax.rem(self.tp + d, self.ntp)}
+    def owner(self, piece):
+        y, zb = piece // NZB, piece % NZB
+        e = lax.rem(y - self.y + NY, NY) * NZB + lax.rem(zb - self.zb + NZB, NZB)
+        return e, {"ctx": (self.za * NZB + zb) * NY + y}
+
+    def other_core(self):
+        return {"tp": self.tp + 1 - 2 * (self.tp % 2)}
+
+    def along_x(self, d):
+        return {"tp": lax.rem(self.tp + 2 * d, self.ntp)}
 
 
 def exchange(at, fill, q_ref, k_ref, v_ref, g_ref, first, hn, hp, vbuf, tails, counts,
@@ -76,7 +91,7 @@
 
     barrier = pltpu.get_barrier_semaphore()
     partners = [at.along_y(d) for d in range(1, NY)] + [at.along_z(d) for d in range(1, nz)] + [at.step(1), at.step(-1)]
-    partners += [at.near(e)[1] for e in range(1, NEAREST)] + [at.along_tp(d) for d in range(1, at.ntp)]
+    partners += [at.near(e)[1] for e in range(1, NEAREST)] + [at.other_core()] + [at.along_x(d) for d in range(1, at.ntp // 2)]
     for device in partners:
         pl.semaphore_signal(barrier, inc=1, device_id=device, device_id_type=MESH)
     counts[at.z, at.y] = jnp.full((1, LANES), fill, I32)
@@ -84,20 +99,19 @@
 
     own = counts.at[at.z, at.y]
     ycopies = [mesh_copy(own, own, ysend.at[d], yrecv.at[d], at.along_y(d)) for d in range(1, NY)]
-    copies = []
-    row = 0
-    for i, (ref, count) in enumerate(((q_ref, HALO), (g_ref, HALO), (k_ref, NEAR), (v_ref, NEAR))):
-        copies.append(mesh_copy(ref.at[pl.ds(0, count)], hp.at[pl.ds(row, count)], hsend.at[i], hrecv.at[i], at.step(-1)))
-        row += count
-    row = 0
-    for i, count in enumerate((HALO, HALO, NEAR)):
-        loads[i].wait()
-        slot = lax.broadcasted_iota(I32, (count, rows), 0) + (fill - count)
-        pick = (slot == lax.broadcasted_iota(I32, (count, rows), 1)).astype(F32).astype(BF16)
-        tails[row:row + count, :] = jnp.dot(pick, vbuf[i], preferred_element_type=F32).astype(BF16)
-        part = pl.ds(row, count)
-        copies.append(mesh_copy(tails.at[part], hn.at[part], hsend.at[4 + i], hrecv.at[4 + i], at.step(1)))
-        row += count
+    for part in range(len(PARTS)):
+        for c in head_copies(at, part, q_ref, k_ref, v_ref, g_ref, hp, hsend, hrecv):
+            c.start()
+        row = 0
+        for i, count in enumerate(TAILS):
+            if part == 0:
+                loads[i].wait()
+                slot = lax.broadcasted_iota(I32, (count, rows), 0) + (fill - count)
+                pick = (slot == lax.broadcasted_iota(I32, (count, rows), 1)).astype(F32).astype(BF16)
+                tails[row:row + count, :] = jnp.dot(pick, vbuf[i], preferred_element_type=F32).astype(BF16)
+            row += count
+        for c in tail_copies(at, part, tails, hn, hsend, hrecv):
+            c.start()
     for c in ycopies:
         c.wait()
     own = counts.at[at.z]
@@ -106,18 +120,36 @@
         c.wait()
     shard = lax.broadcasted_iota(I32, counts.shape, 0) * NY + lax.broadcasted_iota(I32, counts.shape, 1)
     first[...] = jnp.sum(jnp.where(shard < at.me, counts[...], 0), axis=(0, 1))
-    for c in copies:
-        c.wait()
+
+
+def head_copies(at, part, q_ref, k_ref, v_ref, g_ref, hp, hsend, hrecv):
+    copies, row = [], 0
+    cols = pl.ds(PARTS[part][0] * LANES, (PARTS[part][1] - PARTS[part][0]) * LANES)
+    for i, (ref, count) in enumerate(((q_ref, HALO), (g_ref, HALO), (k_ref, NEAR), (v_ref, NEAR))):
+        copies.append(pltpu.make_async_remote_copy(
+            src_ref=ref.at[pl.ds(0, count), cols], dst_ref=hp.at[pl.ds(row, count), cols],
+            send_sem=hsend.at[part, i], recv_sem=hrecv.at[part, i], device_id=at.step(-1), device_id_type=MESH))
+        row += count
+    return copies
+
+
+def tail_copies(at, part, tails, hn, hsend, hrecv):
+    copies, row = [], 0
+    cols = pl.ds(PARTS[part][0] * LANES, (PARTS[part][1] - PARTS[part][0]) * LANES)
+    for i, count in enumerate(TAILS):
+        rows = pl.ds(row, count)
+        copies.append(pltpu.make_async_remote_copy(
+            src_ref=tails.at[rows, cols], dst_ref=hn.at[rows, cols],
+            send_sem=hsend.at[part, 4 + i], recv_sem=hrecv.at[part, 4 + i], device_id=at.step(1), device_id_type=MESH))
+        row += count
+    return copies
 
 
 def sum_shards(at, params, raw, got, parts, full, squares, s1, r1, s2, r2, s3, r3, s4, r4, out_ref):
     mine = at.y * NZB + at.zb
-    copies = []
     for e in range(1, NEAREST):
         piece, device = at.near(e)
-        copies.append(mesh_copy(raw.at[piece], got.at[e], s1.at[e], r1.at[e], device))
-    for c in copies:
-        c.wait()
+        piece_copy(raw, got, s1, r1, piece, e, device).wait()
     acc = raw[mine]
     for e in range(1, NEAREST):
         acc = acc + got[e]
@@ -138,19 +170,22 @@
     for i in range(NEAREST):
         square = square + full[i] * full[i]
     square = jnp.sum(jnp.sum(square, axis=0, keepdims=True), axis=1, keepdims=True)
-    squares[at.tp] = jnp.broadcast_to(square, (1, LANES))
-    own = squares.at[at.tp]
-    copies = [mesh_copy(own, own, s4.at[d], r4.at[d], at.along_tp(d)) for d in range(1, at.ntp)]
+    chip, core = at.tp // 2, at.tp % 2
+    squares[chip, core] = jnp.broadcast_to(square, (1, LANES))
+    own = squares.at[chip, core]
+    mesh_copy(own, own, s4.at[0], r4.at[0], at.other_core()).wait()
+    own = squares.at[chip]
+    copies = [mesh_copy(own, own, s4.at[d], r4.at[d], at.along_x(d)) for d in range(1, at.ntp // 2)]
     for c in copies:
         c.wait()
-    factor = lax.rsqrt(jnp.sum(squares[...], axis=0) / params + 1e-06)
+    factor = lax.rsqrt(jnp.sum(squares[...], axis=(0, 1)) / params + 1e-06)
     for i in range(NEAREST):
         out_ref[i] = full[i] * factor
 
 
 def mix_kernel(nz, ntp, params, fill_ref, docs_ref, qw_ref, kw_ref, vw_ref, gw_ref, q_ref, k_ref, v_ref, g_ref, ft_ref, taps_ref, skip_ref,
                ho_ref, qg_ref, kg_ref, vg_ref, pk_ref,
-               qx, kx, vx, gw, query, keys, values, qb, kb, vb, m, gx, mown, dist, near, maskf, maskb, maskp, shift, taps,
+               qx, kx, vx, gw, query, keys, values, qb, kb, vb, m, gx, mown, dist, near, maskf, maskb, maskp, shift, taps, qo, ko, vo,
                first_row, hn, hp, vbuf, tails, counts, raw, got, parts, full, squares,
                load_sem, ysend, yrecv, zsend, zrecv, hsend, hrecv, s1, r1, s2, r2, s3, r3, s4, r4):
     step = pl.program_id(0)
@@ -204,6 +239,15 @@
         gx[WIN:, :] = jnp.zeros((gx.shape[0] - WIN, LANES), BF16)
         taps[...] = taps_ref[...].astype(F32)
 
+    for part, (begin, _) in enumerate(PARTS):
+
+        @pl.when(step == begin)
+        def _():
+            for c in head_copies(peers, part, qw_ref, kw_ref, vw_ref, gw_ref, hp, hsend, hrecv):
+                c.wait()
+            for c in tail_copies(peers, part, tails, hn, hsend, hrecv):
+                c.wait()
+
     def own_or_next(ref, moved, begin, count):
         slot = lax.broadcasted_iota(I32, (count, LANES), 0) + begin
         return jnp.where(slot < fill, ref[begin:begin + count, :].astype(F32), moved)
@@ -221,7 +265,7 @@
         out[off + 192:off + 256, :] = own_or_next(ref, moved[0:64], 192, 64)
         out[off + 256:off + 192 + moved.shape[0], :] = moved[64:]
 
-    feat = [ft_ref[w].astype(F32) for w in range(3)]
+    feat = [ft_ref[w, :, lanes].astype(F32) for w in range(3)]
     block = 16
 
     def featurize(window, at, far, w):
@@ -272,7 +316,7 @@
     for b, count in blocks:
         at = 128 * b
         gated = acc[b] + skip * m[MSLOT + at:MSLOT + at + count, :].astype(F32)
-        qb[at:at + count, :] = (gw[at:at + count, :] * gated).astype(BF16).astype(F32)
+        qb[step, at:at + count, :] = (gw[at:at + count, :] * gated).astype(BF16).astype(F32)
         if b < 2:
             inside = lax.broadcasted_iota(I32, (count, LANES), 0) + at < fill
             ho_ref[at:at + count, :] = jnp.where(inside, query[at:at + count, :] * gated, 0.0).astype(BF16)
@@ -297,32 +341,55 @@
     for b, count in blocks:
         at = 128 * b
         back = acc[b] + skip * gx[at:at + count, :].astype(F32)
-        kb[at:at + count, :] = (back * values[at:at + count, :]).astype(BF16).astype(F32)
-        vb[at:at + count, :] = (back * keys[at:at + count, :]).astype(BF16).astype(F32)
+        kb[step, at:at + count, :] = (back * values[at:at + count, :]).astype(BF16).astype(F32)
+        vb[step, at:at + count, :] = (back * keys[at:at + count, :]).astype(BF16).astype(F32)
 
     slot = lax.broadcasted_iota(I32, (rows, LANES), 0)
     both = m[MSLOT:MSLOT + rows, :].astype(F32) * gx[0:rows, :].astype(F32)
     skip_row = jnp.sum(jnp.where(slot < fill, both, 0.0), axis=0, keepdims=True)
     feat_rows = []
-    for w, (back, window, off, out) in enumerate(((qb, qx, QOFF, qg_ref), (kb, kx, OFF, kg_ref), (vb, vx, OFF, vg_ref))):
+    for w, (back, window, off) in enumerate(((qb, qx, QOFF), (kb, kx, OFF), (vb, vx, OFF))):
         sums = [jnp.zeros((block, LANES), F32) for _ in range(SHORT)]
         for s in range(0, rows, block):
             reach = near[s:s + block, :]
             source = window[off + s:off + s + block, :]
-            total = jnp.zeros((block, LANES), F32)
             for j in range(SHORT):
-                later = jnp.where(reach >= j, back[s + j:s + j + block, :], 0.0)
-                total = total + feat[w][j:j + 1, :] * later
+                later = jnp.where(reach >= j, back[step, s + j:s + j + block, :], 0.0)
                 sums[j] = sums[j] + source * later
-            out[s:s + block, :] = total.astype(BF16)
         feat_rows += [jnp.sum(x, axis=0, keepdims=True) for x in sums]
     packed = jnp.concatenate(mix_rows + [skip_row] + feat_rows + [jnp.zeros((2, LANES), F32)], axis=0)
-    raw[2 * step] = packed[0:16]
-    raw[2 * step + 1] = packed[16:32]
+    for i in range(2):
+        piece = 2 * step + i
+        raw[piece] = packed[16 * i:16 * i + 16]
+        e, device = peers.owner(piece)
+
+        @pl.when(e != 0)
+        def _():
+            piece_copy(raw, got, s1, r1, piece, e, device).start()
 
     @pl.when(step == pl.num_programs(0) - 1)
     def _():
+        outs = []
+        for w, (back, ref, hbm) in enumerate(((qb, qo, qg_ref), (kb, ko, kg_ref), (vb, vo, vg_ref))):
+
+            def chunk(i, carry):
+                cols = pl.ds(pl.multiple_of(i * LANES, LANES), LANES)
+                weight = ft_ref[w, :, cols].astype(F32)
+                for s in range(0, rows, block):
+                    reach = near[s:s + block, :]
+                    acc = jnp.zeros((block, LANES), F32)
+                    for j in range(SHORT):
+                        later = jnp.where(reach >= j, back[i, s + j:s + j + block, :], 0.0)
+                        acc = acc + weight[j:j + 1, :] * later
+                    ref[s:s + block, cols] = acc.astype(BF16)
+                return carry
+
+            lax.fori_loop(0, pl.num_programs(0), chunk, 0)
+            outs.append(pltpu.make_async_copy(ref, hbm, load_sem.at[w]))
+            outs[w].start()
         sum_shards(peers, params, raw, got, parts, full, squares, s1, r1, s2, r2, s3, r3, s4, r4, pk_ref)
+        for c in outs:
+            c.wait()
 
 
 def mix_call(nz, ntp, params, fill, docs, q, k, v, g, ft, taps, skip):
@@ -339,8 +406,8 @@
         out_shape=tuple(jax.ShapeDtypeStruct((rows, ch), BF16) for _ in range(4))
         + (jax.ShapeDtypeStruct((NEAREST, *piece), F32),),
         in_specs=[smem, smem, hbm, hbm, hbm, hbm, col(rows), col(rows), col(rows), col(rows),
-                  pl.BlockSpec((3, SHORT, LANES), lambda i: (0, 0, i)), pl.BlockSpec(taps.shape, lambda i: (0, 0)), col(1)],
-        out_specs=(col(rows), col(rows), col(rows), col(rows), pl.BlockSpec((NEAREST, *piece), lambda i: (0, 0, 0))),
+                  pl.BlockSpec(ft.shape, lambda i: (0, 0, 0)), pl.BlockSpec(taps.shape, lambda i: (0, 0)), col(1)],
+        out_specs=(col(rows), hbm, hbm, hbm, pl.BlockSpec((NEAREST, *piece), lambda i: (0, 0, 0))),
         scratch_shapes=[
             pltpu.VMEM((QOFF + WIN, LANES), F32),
             pltpu.VMEM((OFF + OUT, LANES), F32),
@@ -349,9 +416,9 @@
             pltpu.VMEM((rows, LANES), F32),
             pltpu.VMEM((OUT, LANES), F32),
             pltpu.VMEM((OUT, LANES), F32),
-            pltpu.VMEM((OUT, LANES), F32),
-            pltpu.VMEM((OUT, LANES), F32),
-            pltpu.VMEM((OUT, LANES), F32),
+            pltpu.VMEM((steps, OUT, LANES), F32),
+            pltpu.VMEM((steps, OUT, LANES), F32),
+            pltpu.VMEM((steps, OUT, LANES), F32),
             pltpu.VMEM((512, LANES), BF16),
             pltpu.VMEM((512, LANES), BF16),
             pltpu.VMEM((rows, LANES), BF16),
@@ -362,6 +429,9 @@
             pltpu.VMEM((rows, 256), F32),
             pltpu.VMEM((WIN - 192, HALO), BF16),
             pltpu.VMEM(taps.shape, F32),
+            pltpu.VMEM((rows, ch), BF16),
+            pltpu.VMEM((rows, ch), BF16),
+            pltpu.VMEM((rows, ch), BF16),
             pltpu.VMEM((1, LANES), I32),
             pltpu.VMEM((2 * HALO + NEAR, ch), BF16),
             pltpu.VMEM((2 * HALO + 2 * NEAR, ch), BF16),
@@ -372,8 +442,8 @@
             pltpu.VMEM((NEAREST, *piece), F32),
             pltpu.VMEM((nz // NZB, *piece), F32),
             pltpu.VMEM((NEAREST, *piece), F32),
-            pltpu.VMEM((ntp, 1, LANES), F32),
-            dma((3,)), dma((NY,)), dma((NY,)), dma((nz,)), dma((nz,)), dma((7,)), dma((7,)),
+            pltpu.VMEM((ntp // 2, 2, 1, LANES), F32),
+            dma((3,)), dma((NY,)), dma((NY,)), dma((nz,)), dma((nz,)), dma((len(PARTS), 7)), dma((len(PARTS), 7)),
             dma((NEAREST,)), dma((NEAREST,)), dma((nz // NZB,)), dma((nz // NZB,)), dma((NEAREST,)), dma((NEAREST,)),
             dma((ntp,)), dma((ntp,)),
         ],
@@ -383,36 +453,42 @@
 
 
 def place_kernel(*refs):
-    pk_ref, mix_ref, skip_ref, feat_ref = refs[4], *refs[9:]
-    for source, out in zip(refs[:4], refs[5:9]):
-        out[...] = source[...]
-
-    @pl.when(pl.program_id(0) == 0)
-    def _():
-        for k in range(pk_ref.shape[0] // 2):
-            lanes = slice(LANES * k, LANES * k + LANES)
-            mix_ref[8 * k:8 * k + 8, :] = pk_ref[2 * k, 0:8]
-            skip_ref[:, lanes] = pk_ref[2 * k, 8:9]
-            for w in range(3):
-                for j in range(SHORT):
-                    r = 9 + SHORT * w + j
-                    feat_ref[w, j:j + 1, lanes] = pk_ref[2 * k + r // 16, r % 16:r % 16 + 1]
+    big, pk_ref, outs = refs[:4], refs[4], refs[5:9]
+    mix_ref, skip_ref, feat_ref, held, load, store = refs[9:]
+    half = held.shape[1] // 2
+    moves = [(i, j, pl.ds(half * j, half)) for j in range(2) for i in range(4)]
+    loads = [pltpu.make_async_copy(big[i].at[part], held.at[i, part], load.at[i, j]) for i, j, part in moves]
+    stores = [pltpu.make_async_copy(held.at[i, part], outs[i].at[part], store.at[i, j]) for i, j, part in moves]
+    for c in loads:
+        c.start()
+    for c, d in zip(loads, stores):
+        c.wait()
+        d.start()
+    for k in range(pk_ref.shape[0] // 2):
+        lanes = slice(LANES * k, LANES * k + LANES)
+        mix_ref[8 * k:8 * k + 8, :] = pk_ref[2 * k, 0:8]
+        skip_ref[:, lanes] = pk_ref[2 * k, 8:9]
+        for w in range(3):
+            for j in range(SHORT):
+                r = 9 + SHORT * w + j
+                feat_ref[w, j:j + 1, lanes] = pk_ref[2 * k + r // 16, r % 16:r % 16 + 1]
+    for d in stores:
+        d.wait()
 
 
 def place_call(big, pk, groups):
     rows, ch = big[0].shape
-    whole = lambda *shape: pl.BlockSpec(shape, lambda i: (0,) * len(shape))
-    part = pl.BlockSpec((64, ch), lambda i: (i, 0))
+    vmem, hbm = pl.BlockSpec(memory_space=pltpu.VMEM), pl.BlockSpec(memory_space=pl.ANY)
     return pl.pallas_call(
         place_kernel,
-        grid=(rows // 64,),
         out_shape=tuple(jax.ShapeDtypeStruct((rows, ch), BF16) for _ in range(4)) + (
             jax.ShapeDtypeStruct((groups, FILT), F32),
             jax.ShapeDtypeStruct((1, ch), F32),
             jax.ShapeDtypeStruct((3, SHORT, ch), F32),
         ),
-        in_specs=[part] * 4 + [whole(*pk.shape)],
-        out_specs=(part,) * 4 + (whole(groups, FILT), whole(1, ch), whole(3, SHORT, ch)),
+        in_specs=[hbm] * 4 + [vmem],
+        out_specs=(hbm,) * 4 + (vmem,) * 3,
+        scratch_shapes=[pltpu.VMEM((4, rows, ch), BF16), pltpu.SemaphoreType.DMA((4, 2)), pltpu.SemaphoreType.DMA((4, 2))],
         compiler_params=pltpu.CompilerParams(vmem_limit_bytes=60 << 20),
         name="place",
     )(*big, pk)

time: 88.6 us -> 87 us (0.982)
  Pallas kernels: 87 us -> 85.5 us
    pallas_call x1, Pallas kernels: 83 us -> 81.6 us  [mix_call(): pl.pallas_call(lambda *refs: mix_kernel(nz, ntp, params, *refs), grid=(st...]
where the time goes in v3:
time: 87 us; the launch traced here: 86.8 us
  Pallas kernels  85.5 us (98%)
  between operations  1.29 us (1%)
    pallas_call x1, Pallas kernels, mix_call(): pl.pallas_call(lambda *refs: mix_kernel(nz, ntp, params, *refs), grid=(st...  81.6 us
    pallas_call x1, Pallas kernels, place_call(): pl.pallas_call(place_kernel, out_shape=tuple((jax.ShapeDtypeStruct((rows,...  3.95 us

profile of v3, /device:TPU:1, one launch (start us, length us, event | category | flops | bytes accessed | tf_op | source)
XLA Modules:
  0.0 86.8 jit_solution(16765042941911664020)
XLA Ops:
  1.3 81.6 %mix.1 = (bf16[256,1024]{1,0:T(8,128)(2,1)}, bf16[256,1024]{1,0:T(8,128)(2,1)}, bf16[256,1024]{1,0:T(8,128)(2,1)}, bf16[256,1024]{1,0:T(8,128)(2,1)}, f32[16,16,128]{2,1,0:T(8,128)}) custom-call(s32[1]{0:T(128)S(6)} %copy.16.refs_0_, s32[4]{0:T(128)} %refs_1_.1, bf16[256,1024]{1,0:T(8,128)(2,1)} %refs_6_.1, bf16[256,1024]{1,0:T(8,128)(2,1)} %refs_7_.1, ...), custom_call_target="tpu_custom_call" | custom-call | tf_op jit(solution)/shard_map/mix/pallas_call | solution.py:403
  82.8 4.0 %place.1 = (bf16[256,1024]{1,0:T(8,128)(2,1)}, bf16[256,1024]{1,0:T(8,128)(2,1)}, bf16[256,1024]{1,0:T(8,128)(2,1)}, bf16[256,1024]{1,0:T(8,128)(2,1)}, f32[64,1...) custom-call(bf16[256,1024]{1,0:T(8,128)(2,1)} %get-tuple-element.19.refs_0_, ...), custom_call_target="tpu_custom_call" | custom-call | tf_op jit(solution)/shard_map/place/pallas_call | solution.py:482

commit v4 on v3

--- a/solution.py
+++ b/solution.py
@@ -84,7 +84,7 @@
              load_sem, ysend, yrecv, zsend, zrecv, hsend, hrecv):
     nz, rows = at.nz, q_ref.shape[0]
     loads = []
-    for i, ref in enumerate((k_ref, v_ref, q_ref)):
+    for i, ref in enumerate((q_ref, k_ref, v_ref, g_ref)):
         c = pltpu.make_async_copy(ref, vbuf.at[i], load_sem.at[i])
         c.start()
         loads.append(c)
@@ -99,25 +99,29 @@
 
     own = counts.at[at.z, at.y]
     ycopies = [mesh_copy(own, own, ysend.at[d], yrecv.at[d], at.along_y(d)) for d in range(1, NY)]
-    for part in range(len(PARTS)):
-        for c in head_copies(at, part, q_ref, k_ref, v_ref, g_ref, hp, hsend, hrecv):
-            c.start()
-        row = 0
-        for i, count in enumerate(TAILS):
-            if part == 0:
-                loads[i].wait()
-                slot = lax.broadcasted_iota(I32, (count, rows), 0) + (fill - count)
-                pick = (slot == lax.broadcasted_iota(I32, (count, rows), 1)).astype(F32).astype(BF16)
-                tails[row:row + count, :] = jnp.dot(pick, vbuf[i], preferred_element_type=F32).astype(BF16)
-            row += count
-        for c in tail_copies(at, part, tails, hn, hsend, hrecv):
-            c.start()
+    for c in head_copies(at, 0, q_ref, k_ref, v_ref, g_ref, hp, hsend, hrecv):
+        c.start()
+    row = 0
+    for i, count in zip((1, 2, 0), TAILS):
+        loads[i].wait()
+        slot = lax.broadcasted_iota(I32, (count, rows), 0) + (fill - count)
+        pick = (slot == lax.broadcasted_iota(I32, (count, rows), 1)).astype(F32).astype(BF16)
+        tails[row:row + count, :] = jnp.dot(pick, vbuf[i], preferred_element_type=F32).astype(BF16)
+        row += count
+    for c in tail_copies(at, 0, tails, hn, hsend, hrecv):
+        c.start()
     for c in ycopies:
         c.wait()
     own = counts.at[at.z]
     zcopies = [mesh_copy(own, own, zsend.at[d], zrecv.at[d], at.along_z(d)) for d in range(1, nz)]
+    for part in range(1, len(PARTS)):
+        for c in head_copies(at, part, q_ref, k_ref, v_ref, g_ref, hp, hsend, hrecv):
+            c.start()
+        for c in tail_copies(at, part, tails, hn, hsend, hrecv):
+            c.start()
     for c in zcopies:
         c.wait()
+    loads[3].wait()
     shard = lax.broadcasted_iota(I32, counts.shape, 0) * NY + lax.broadcasted_iota(I32, counts.shape, 1)
     first[...] = jnp.sum(jnp.where(shard < at.me, counts[...], 0), axis=(0, 1))
 
@@ -145,7 +149,7 @@
     return copies
 
 
-def sum_shards(at, params, raw, got, parts, full, squares, s1, r1, s2, r2, s3, r3, s4, r4, out_ref):
+def sum_shards(at, params, meanwhile, raw, got, parts, full, squares, s1, r1, s2, r2, s3, r3, s4, r4, out_ref):
     mine = at.y * NZB + at.zb
     for e in range(1, NEAREST):
         piece, device = at.near(e)
@@ -156,6 +160,7 @@
     parts[at.za] = acc
     own = parts.at[at.za]
     copies = [mesh_copy(own, own, s2.at[d], r2.at[d], at.far(d)) for d in range(1, at.nza)]
+    meanwhile()
     for c in copies:
         c.wait()
     acc = parts[0]
@@ -183,9 +188,9 @@
         out_ref[i] = full[i] * factor
 
 
-def mix_kernel(nz, ntp, params, fill_ref, docs_ref, qw_ref, kw_ref, vw_ref, gw_ref, q_ref, k_ref, v_ref, g_ref, ft_ref, taps_ref, skip_ref,
+def mix_kernel(nz, ntp, params, fill_ref, docs_ref, q_ref, k_ref, v_ref, g_ref, ft_ref, taps_ref, skip_ref,
                ho_ref, qg_ref, kg_ref, vg_ref, pk_ref,
-               qx, kx, vx, gw, query, keys, values, qb, kb, vb, m, gx, mown, dist, near, maskf, maskb, maskp, shift, taps, qo, ko, vo,
+               qx, kx, vx, gw, query, keys, values, qb, kb, vb, m, gx, mown, dist, near, maskf, maskb, maskp, shift, taps, vout,
                first_row, hn, hp, vbuf, tails, counts, raw, got, parts, full, squares,
                load_sem, ysend, yrecv, zsend, zrecv, hsend, hrecv, s1, r1, s2, r2, s3, r3, s4, r4):
     step = pl.program_id(0)
@@ -196,7 +201,7 @@
 
     @pl.when(step == 0)
     def _():
-        exchange(peers, fill, qw_ref, kw_ref, vw_ref, gw_ref, first_row, hn, hp, vbuf, tails, counts,
+        exchange(peers, fill, q_ref, k_ref, v_ref, g_ref, first_row, hn, hp, vbuf, tails, counts,
                  load_sem, ysend, yrecv, zsend, zrecv, hsend, hrecv)
         begin_rows = [docs_ref[i] - first_row[...] for i in range(docs_ref.shape[0])]
         end = jnp.where(last, fill, BIG)
@@ -243,14 +248,14 @@
 
         @pl.when(step == begin)
         def _():
-            for c in head_copies(peers, part, qw_ref, kw_ref, vw_ref, gw_ref, hp, hsend, hrecv):
+            for c in head_copies(peers, part, q_ref, k_ref, v_ref, g_ref, hp, hsend, hrecv):
                 c.wait()
             for c in tail_copies(peers, part, tails, hn, hsend, hrecv):
                 c.wait()
 
-    def own_or_next(ref, moved, begin, count):
+    def own_or_next(i, moved, begin, count):
         slot = lax.broadcasted_iota(I32, (count, LANES), 0) + begin
-        return jnp.where(slot < fill, ref[begin:begin + count, :].astype(F32), moved)
+        return jnp.where(slot < fill, vbuf[i, begin:begin + count, lanes].astype(F32), moved)
 
     lanes = pl.ds(pl.multiple_of(step * LANES, LANES), LANES)
     kx[0:OFF, :] = hn[0:HALO, lanes].astype(F32)
@@ -260,9 +265,10 @@
     moved_g = jnp.dot(shift[...], hp[HALO:2 * HALO, lanes], preferred_element_type=F32)
     moved_k = jnp.dot(shift[0:80, 0:NEAR], hp[2 * HALO:2 * HALO + NEAR, lanes], preferred_element_type=F32)
     moved_v = jnp.dot(shift[0:80, 0:NEAR], hp[2 * HALO + NEAR:2 * HALO + 2 * NEAR, lanes], preferred_element_type=F32)
-    for ref, out, off, moved in ((q_ref, qx, QOFF, moved_q), (g_ref, gw, 0, moved_g), (k_ref, kx, OFF, moved_k), (v_ref, vx, OFF, moved_v)):
-        out[off:off + 192, :] = ref[0:192, :].astype(F32)
-        out[off + 192:off + 256, :] = own_or_next(ref, moved[0:64], 192, 64)
+    windows = ((qx, QOFF, moved_q), (kx, OFF, moved_k), (vx, OFF, moved_v), (gw, 0, moved_g))
+    for i, (out, off, moved) in enumerate(windows):
+        out[off:off + 192, :] = vbuf[i, 0:192, lanes].astype(F32)
+        out[off + 192:off + 256, :] = own_or_next(i, moved[0:64], 192, 64)
         out[off + 256:off + 192 + moved.shape[0], :] = moved[64:]
 
     feat = [ft_ref[w, :, lanes].astype(F32) for w in range(3)]
@@ -304,7 +310,7 @@
         return pltpu.roll(jnp.broadcast_to(row, (FILT, FILT)), 0, 1, stride=1, stride_axis=0)
 
     blocks = ((0, 128), (1, 128), (2, 16))
-    skip = skip_ref[...]
+    skip = skip_ref[:, lanes]
 
     acc = [jnp.zeros((count, LANES), F32) for _, count in blocks]
     for g in range(8):
@@ -319,7 +325,7 @@
         qb[step, at:at + count, :] = (gw[at:at + count, :] * gated).astype(BF16).astype(F32)
         if b < 2:
             inside = lax.broadcasted_iota(I32, (count, LANES), 0) + at < fill
-            ho_ref[at:at + count, :] = jnp.where(inside, query[at:at + count, :] * gated, 0.0).astype(BF16)
+            vout[0, at:at + count, lanes] = jnp.where(inside, query[at:at + count, :] * gated, 0.0).astype(BF16)
 
     acc = [jnp.zeros((count, LANES), F32) for _, count in blocks]
     mix_rows = []
@@ -369,25 +375,28 @@
 
     @pl.when(step == pl.num_programs(0) - 1)
     def _():
-        outs = []
-        for w, (back, ref, hbm) in enumerate(((qb, qo, qg_ref), (kb, ko, kg_ref), (vb, vo, vg_ref))):
-
-            def chunk(i, carry):
-                cols = pl.ds(pl.multiple_of(i * LANES, LANES), LANES)
-                weight = ft_ref[w, :, cols].astype(F32)
-                for s in range(0, rows, block):
-                    reach = near[s:s + block, :]
-                    acc = jnp.zeros((block, LANES), F32)
-                    for j in range(SHORT):
-                        later = jnp.where(reach >= j, back[i, s + j:s + j + block, :], 0.0)
-                        acc = acc + weight[j:j + 1, :] * later
-                    ref[s:s + block, cols] = acc.astype(BF16)
-                return carry
-
-            lax.fori_loop(0, pl.num_programs(0), chunk, 0)
-            outs.append(pltpu.make_async_copy(ref, hbm, load_sem.at[w]))
-            outs[w].start()
-        sum_shards(peers, params, raw, got, parts, full, squares, s1, r1, s2, r2, s3, r3, s4, r4, pk_ref)
+        outs = [pltpu.make_async_copy(vout.at[i], ref, load_sem.at[i]) for i, ref in enumerate((ho_ref, qg_ref, kg_ref, vg_ref))]
+
+        def meanwhile():
+            outs[0].start()
+            for w, back in enumerate((qb, kb, vb)):
+
+                def chunk(i, carry):
+                    cols = pl.ds(pl.multiple_of(i * LANES, LANES), LANES)
+                    weight = ft_ref[w, :, cols].astype(F32)
+                    for s in range(0, rows, block):
+                        reach = near[s:s + block, :]
+                        acc = jnp.zeros((block, LANES), F32)
+                        for j in range(SHORT):
+                            later = jnp.where(reach >= j, back[i, s + j:s + j + block, :], 0.0)
+                            acc = acc + weight[j:j + 1, :] * later
+                        vout[1 + w, s:s + block, cols] = acc.astype(BF16)
+                    return carry
+
+                lax.fori_loop(0, pl.num_programs(0), chunk, 0)
+                outs[1 + w].start()
+
+        sum_shards(peers, params, meanwhile, raw, got, parts, full, squares, s1, r1, s2, r2, s3, r3, s4, r4, pk_ref)
         for c in outs:
             c.wait()
 
@@ -395,7 +404,6 @@
 def mix_call(nz, ntp, params, fill, docs, q, k, v, g, ft, taps, skip):
     rows, ch = q.shape
     steps = ch // LANES
-    col = lambda count: pl.BlockSpec((count, LANES), lambda i: (0, i))
     smem = pl.BlockSpec(memory_space=pltpu.SMEM)
     hbm = pl.BlockSpec(memory_space=pl.ANY)
     dma = pltpu.SemaphoreType.DMA
@@ -405,9 +413,10 @@
         grid=(steps,),
         out_shape=tuple(jax.ShapeDtypeStruct((rows, ch), BF16) for _ in range(4))
         + (jax.ShapeDtypeStruct((NEAREST, *piece), F32),),
-        in_specs=[smem, smem, hbm, hbm, hbm, hbm, col(rows), col(rows), col(rows), col(rows),
-                  pl.BlockSpec(ft.shape, lambda i: (0, 0, 0)), pl.BlockSpec(taps.shape, lambda i: (0, 0)), col(1)],
-        out_specs=(col(rows), hbm, hbm, hbm, pl.BlockSpec((NEAREST, *piece), lambda i: (0, 0, 0))),
+        in_specs=[smem, smem, hbm, hbm, hbm, hbm,
+                  pl.BlockSpec(ft.shape, lambda i: (0, 0, 0)), pl.BlockSpec(taps.shape, lambda i: (0, 0)),
+                  pl.BlockSpec(skip.shape, lambda i: (0, 0))],
+        out_specs=(hbm, hbm, hbm, hbm, pl.BlockSpec((NEAREST, *piece), lambda i: (0, 0, 0))),
         scratch_shapes=[
             pltpu.VMEM((QOFF + WIN, LANES), F32),
             pltpu.VMEM((OFF + OUT, LANES), F32),
@@ -429,13 +438,11 @@
             pltpu.VMEM((rows, 256), F32),
             pltpu.VMEM((WIN - 192, HALO), BF16),
             pltpu.VMEM(taps.shape, F32),
-            pltpu.VMEM((rows, ch), BF16),
-            pltpu.VMEM((rows, ch), BF16),
-            pltpu.VMEM((rows, ch), BF16),
+            pltpu.VMEM((4, rows, ch), BF16),
             pltpu.VMEM((1, LANES), I32),
             pltpu.VMEM((2 * HALO + NEAR, ch), BF16),
             pltpu.VMEM((2 * HALO + 2 * NEAR, ch), BF16),
-            pltpu.VMEM((3, rows, ch), BF16),
+            pltpu.VMEM((4, rows, ch), BF16),
             pltpu.VMEM((2 * HALO + NEAR, ch), BF16),
             pltpu.VMEM((nz, NY, 1, LANES), I32),
             pltpu.VMEM((NEAREST, *piece), F32),
@@ -443,52 +450,59 @@
             pltpu.VMEM((nz // NZB, *piece), F32),
             pltpu.VMEM((NEAREST, *piece), F32),
             pltpu.VMEM((ntp // 2, 2, 1, LANES), F32),
-            dma((3,)), dma((NY,)), dma((NY,)), dma((nz,)), dma((nz,)), dma((len(PARTS), 7)), dma((len(PARTS), 7)),
+            dma((4,)), dma((NY,)), dma((NY,)), dma((nz,)), dma((nz,)), dma((len(PARTS), 7)), dma((len(PARTS), 7)),
             dma((NEAREST,)), dma((NEAREST,)), dma((nz // NZB,)), dma((nz // NZB,)), dma((NEAREST,)), dma((NEAREST,)),
             dma((ntp,)), dma((ntp,)),
         ],
         compiler_params=pltpu.CompilerParams(collective_id=0, has_side_effects=True, vmem_limit_bytes=60 << 20),
         name="mix",
-    )(fill, docs, q, k, v, g, q, k, v, g, ft, taps, skip)
+    )(fill, docs, q, k, v, g, ft, taps, skip)
 
 
 def place_kernel(*refs):
-    big, pk_ref, outs = refs[:4], refs[4], refs[5:9]
-    mix_ref, skip_ref, feat_ref, held, load, store = refs[9:]
+    big, pk_ref, outs, small = refs[:4], refs[4], refs[5:9], refs[9:12]
+    held, pk, mix, skip, feat, load, store = refs[12:]
     half = held.shape[1] // 2
     moves = [(i, j, pl.ds(half * j, half)) for j in range(2) for i in range(4)]
+    first = pltpu.make_async_copy(pk_ref, pk, load.at[4, 0])
+    first.start()
     loads = [pltpu.make_async_copy(big[i].at[part], held.at[i, part], load.at[i, j]) for i, j, part in moves]
     stores = [pltpu.make_async_copy(held.at[i, part], outs[i].at[part], store.at[i, j]) for i, j, part in moves]
     for c in loads:
         c.start()
+    first.wait()
+    for k in range(pk.shape[0] // 2):
+        lanes = slice(LANES * k, LANES * k + LANES)
+        mix[8 * k:8 * k + 8, :] = pk[2 * k, 0:8]
+        skip[:, lanes] = pk[2 * k, 8:9]
+        for w in range(3):
+            for j in range(SHORT):
+                r = 9 + SHORT * w + j
+                feat[w, j:j + 1, lanes] = pk[2 * k + r // 16, r % 16:r % 16 + 1]
+    for i, source in enumerate((mix, skip, feat)):
+        c = pltpu.make_async_copy(source, small[i], store.at[4 + i, 0])
+        c.start()
+        stores.append(c)
     for c, d in zip(loads, stores):
         c.wait()
         d.start()
-    for k in range(pk_ref.shape[0] // 2):
-        lanes = slice(LANES * k, LANES * k + LANES)
-        mix_ref[8 * k:8 * k + 8, :] = pk_ref[2 * k, 0:8]
-        skip_ref[:, lanes] = pk_ref[2 * k, 8:9]
-        for w in range(3):
-            for j in range(SHORT):
-                r = 9 + SHORT * w + j
-                feat_ref[w, j:j + 1, lanes] = pk_ref[2 * k + r // 16, r % 16:r % 16 + 1]
     for d in stores:
         d.wait()
 
 
 def place_call(big, pk, groups):
     rows, ch = big[0].shape
-    vmem, hbm = pl.BlockSpec(memory_space=pltpu.VMEM), pl.BlockSpec(memory_space=pl.ANY)
+    hbm = pl.BlockSpec(memory_space=pl.ANY)
+    small = ((groups, FILT), (1, ch), (3, SHORT, ch))
     return pl.pallas_call(
         place_kernel,
-        out_shape=tuple(jax.ShapeDtypeStruct((rows, ch), BF16) for _ in range(4)) + (
-            jax.ShapeDtypeStruct((groups, FILT), F32),
-            jax.ShapeDtypeStruct((1, ch), F32),
-            jax.ShapeDtypeStruct((3, SHORT, ch), F32),
-        ),
-        in_specs=[hbm] * 4 + [vmem],
-        out_specs=(hbm,) * 4 + (vmem,) * 3,
-        scratch_shapes=[pltpu.VMEM((4, rows, ch), BF16), pltpu.SemaphoreType.DMA((4, 2)), pltpu.SemaphoreType.DMA((4, 2))],
+        out_shape=tuple(jax.ShapeDtypeStruct((rows, ch), BF16) for _ in range(4))
+        + tuple(jax.ShapeDtypeStruct(shape, F32) for shape in small),
+        in_specs=[hbm] * 5,
+        out_specs=(hbm,) * 7,
+        scratch_shapes=[pltpu.VMEM((4, rows, ch), BF16), pltpu.VMEM(pk.shape, F32)]
+        + [pltpu.VMEM(shape, F32) for shape in small]
+        + [pltpu.SemaphoreType.DMA((5, 2)), pltpu.SemaphoreType.DMA((7, 2))],
         compiler_params=pltpu.CompilerParams(vmem_limit_bytes=60 << 20),
         name="place",
     )(*big, pk)

time: 87 us -> 76.8 us (0.88)
  Pallas kernels: 85.5 us -> 75.3 us
    pallas_call x1, Pallas kernels: 81.6 us -> 72.8 us  [mix_call(): pl.pallas_call(lambda *refs: mix_kernel(nz, ntp, params, *refs), grid=(st...]
    pallas_call x1, Pallas kernels: 3.95 us -> 2.54 us  [place_call(): pl.pallas_call(place_kernel, out_shape=tuple((jax.ShapeDtypeStruct((rows,...]
where the time goes in v4:
time: 76.8 us; the launch traced here: 76.6 us
  Pallas kernels  75.3 us (98%)
  between operations  1.29 us (2%)
    pallas_call x1, Pallas kernels, mix_call(): pl.pallas_call(lambda *refs: mix_kernel(nz, ntp, params, *refs), grid=(st...  72.8 us
    pallas_call x1, Pallas kernels, place_call(): pl.pallas_call(place_kernel, out_shape=tuple((jax.ShapeDtypeStruct((rows,...  2.54 us

profile of v4, /device:TPU:1, one launch (start us, length us, event | category | flops | bytes accessed | tf_op | source)
XLA Modules:
  0.0 76.6 jit_solution(549981728047509297)
XLA Ops:
  1.3 72.8 %mix.1 = (bf16[256,1024]{1,0:T(8,128)(2,1)}, bf16[256,1024]{1,0:T(8,128)(2,1)}, bf16[256,1024]{1,0:T(8,128)(2,1)}, bf16[256,1024]{1,0:T(8,128)(2,1)}, f32[16,16,128]{2,1,0:T(8,128)}) custom-call(s32[1]{0:T(128)S(6)} %copy.16.refs_0_, s32[4]{0:T(128)} %refs_1_.1, bf16[256,1024]{1,0:T(8,128)(2,1)} %refs_2_.1, bf16[256,1024]{1,0:T(8,128)(2,1)} %refs_3_.1, ...), custom_call_target="tpu_custom_call" | custom-call | tf_op jit(solution)/shard_map/mix/pallas_call | solution.py:411
  74.1 2.5 %place.1 = (bf16[256,1024]{1,0:T(8,128)(2,1)}, bf16[256,1024]{1,0:T(8,128)(2,1)}, bf16[256,1024]{1,0:T(8,128)(2,1)}, bf16[256,1024]{1,0:T(8,128)(2,1)}, f32[64,1...) custom-call(bf16[256,1024]{1,0:T(8,128)(2,1)} %get-tuple-element.19.refs_0_, ...), custom_call_target="tpu_custom_call" | custom-call | tf_op jit(solution)/shard_map/place/pallas_call | solution.py:497

commit v5 on v4

--- a/solution.py
+++ b/solution.py
@@ -80,7 +80,7 @@
         return {"tp": lax.rem(self.tp + 2 * d, self.ntp)}
 
 
-def exchange(at, fill, q_ref, k_ref, v_ref, g_ref, first, hn, hp, vbuf, tails, counts,
+def exchange(at, fill, meanwhile, q_ref, k_ref, v_ref, g_ref, first, hn, hp, vbuf, tails, counts,
              load_sem, ysend, yrecv, zsend, zrecv, hsend, hrecv):
     nz, rows = at.nz, q_ref.shape[0]
     loads = []
@@ -91,7 +91,7 @@
 
     barrier = pltpu.get_barrier_semaphore()
     partners = [at.along_y(d) for d in range(1, NY)] + [at.along_z(d) for d in range(1, nz)] + [at.step(1), at.step(-1)]
-    partners += [at.near(e)[1] for e in range(1, NEAREST)] + [at.other_core()] + [at.along_x(d) for d in range(1, at.ntp // 2)]
+    partners += [at.near(e)[1] for e in range(1, NEAREST) if e // NZB and e % NZB] + [at.other_core()] + [at.along_x(d) for d in range(1, at.ntp // 2)]
     for device in partners:
         pl.semaphore_signal(barrier, inc=1, device_id=device, device_id_type=MESH)
     counts[at.z, at.y] = jnp.full((1, LANES), fill, I32)
@@ -119,6 +119,7 @@
             c.start()
         for c in tail_copies(at, part, tails, hn, hsend, hrecv):
             c.start()
+    meanwhile()
     for c in zcopies:
         c.wait()
     loads[3].wait()
@@ -190,7 +191,7 @@
 
 def mix_kernel(nz, ntp, params, fill_ref, docs_ref, q_ref, k_ref, v_ref, g_ref, ft_ref, taps_ref, skip_ref,
                ho_ref, qg_ref, kg_ref, vg_ref, pk_ref,
-               qx, kx, vx, gw, query, keys, values, qb, kb, vb, m, gx, mown, dist, near, maskf, maskb, maskp, shift, taps, vout,
+               qx, kx, vx, gw, query, keys, values, qb, kb, vb, m, gx, mown, dist, near, maskf, maskb, maskp, shift, taps, vout, stack, pairs, fold,
                first_row, hn, hp, vbuf, tails, counts, raw, got, parts, full, squares,
                load_sem, ysend, yrecv, zsend, zrecv, hsend, hrecv, s1, r1, s2, r2, s3, r3, s4, r4):
     step = pl.program_id(0)
@@ -201,7 +202,14 @@
 
     @pl.when(step == 0)
     def _():
-        exchange(peers, fill, q_ref, k_ref, v_ref, g_ref, first_row, hn, hp, vbuf, tails, counts,
+        def meanwhile():
+            r = lax.broadcasted_iota(I32, shift.shape, 0) + 192
+            shift[...] = (r - fill == lax.broadcasted_iota(I32, shift.shape, 1)).astype(F32).astype(BF16)
+            m[MSLOT + OUT:, :] = jnp.zeros((m.shape[0] - MSLOT - OUT, LANES), BF16)
+            gx[WIN:, :] = jnp.zeros((gx.shape[0] - WIN, LANES), BF16)
+            taps[...] = taps_ref[...].astype(F32)
+
+        exchange(peers, fill, meanwhile, q_ref, k_ref, v_ref, g_ref, first_row, hn, hp, vbuf, tails, counts,
                  load_sem, ysend, yrecv, zsend, zrecv, hsend, hrecv)
         begin_rows = [docs_ref[i] - first_row[...] for i in range(docs_ref.shape[0])]
         end = jnp.where(last, fill, BIG)
@@ -225,24 +233,20 @@
             shape = (count, 256)
             a = lax.broadcasted_iota(I32, shape, 0)
             lane = lax.broadcasted_iota(I32, shape, 1)
-            p, source = 128 * b + a, 128 * (b - 1) + lane
-            j = p - source
-            keep = (j >= 0) & (j < FILT) & (source >= doc_begin(p))
+            far = dist[MSLOT + 128 * b:MSLOT + 128 * b + count, :]
+            far = jnp.concatenate([far, far], axis=1)
+            j = a + 128 - lane
+            keep = (j >= 0) & (j < FILT) & (j <= far)
             maskf[128 * b:128 * b + count, :] = keep.astype(F32).astype(BF16)
-            later = 128 * b + lane
-            j = later - p
+            later = 128 * b + lax.broadcasted_iota(I32, (8, 256), 1)
             begin = jnp.where(later < end, doc_begin(later), BIG)
-            keep = (j >= 0) & (j < FILT) & (p >= begin)
+            begin = jnp.broadcast_to(begin[0:1], shape) - 128 * b
+            j = lane - a
+            keep = (j >= 0) & (j < FILT) & (a >= begin)
             maskb[128 * b:128 * b + count, :] = keep.astype(F32).astype(BF16)
             if b < 2:
-                p = 128 * b + 127 - a
-                j = later - p
-                maskp[128 * b:128 * b + count, :] = ((j >= 0) & (j < FILT) & (p >= begin)).astype(F32)
-        r = lax.broadcasted_iota(I32, shift.shape, 0) + 192
-        shift[...] = (r - fill == lax.broadcasted_iota(I32, shift.shape, 1)).astype(F32).astype(BF16)
-        m[MSLOT + OUT:, :] = jnp.zeros((m.shape[0] - MSLOT - OUT, LANES), BF16)
-        gx[WIN:, :] = jnp.zeros((gx.shape[0] - WIN, LANES), BF16)
-        taps[...] = taps_ref[...].astype(F32)
+                j = lane - 127 + a
+                maskp[128 * b:128 * b + count, :] = ((j >= 0) & (j < FILT) & (127 - a >= begin)).astype(F32)
 
     for part, (begin, _) in enumerate(PARTS):
 
@@ -312,13 +316,22 @@
     blocks = ((0, 128), (1, 128), (2, 16))
     skip = skip_ref[:, lanes]
 
-    acc = [jnp.zeros((count, LANES), F32) for _, count in blocks]
-    for g in range(8):
-        circ = circulant(turned[g:g + 1, :]).astype(BF16)
+    def banded(rows8, mask, window):
+        for g in range(8):
+            circ = circulant(rows8[g:g + 1, :]).astype(BF16)
+            circ = jnp.concatenate([circ, circ], axis=1)
+            for b, count in blocks:
+                stack[b, g * count:(g + 1) * count, :] = circ[:count] * mask[128 * b:128 * b + count, :]
+        acc = []
         for b, count in blocks:
-            both = jnp.concatenate([circ[:count], circ[:count]], axis=1) * maskf[128 * b:128 * b + count, :]
-            res = jnp.dot(both, m[128 * b:128 * b + 256, :], preferred_element_type=F32)
-            acc[b] = jnp.where(group_of[:count] == g, res, acc[b])
+            res = jnp.dot(stack[b, 0:8 * count, :], window[128 * b:128 * b + 256, :], preferred_element_type=F32)
+            out = res[0:count]
+            for g in range(1, 8):
+                out = jnp.where(group_of[:count] == g, res[g * count:(g + 1) * count], out)
+            acc.append(out)
+        return acc
+
+    acc = banded(turned, maskf, m)
     for b, count in blocks:
         at = 128 * b
         gated = acc[b] + skip * m[MSLOT + at:MSLOT + at + count, :].astype(F32)
@@ -327,23 +340,22 @@
             inside = lax.broadcasted_iota(I32, (count, LANES), 0) + at < fill
             vout[0, at:at + count, lanes] = jnp.where(inside, query[at:at + count, :] * gated, 0.0).astype(BF16)
 
-    acc = [jnp.zeros((count, LANES), F32) for _, count in blocks]
+    acc = banded(my_taps, maskb, gx)
     mix_rows = []
-    for g in range(8):
-        circ = circulant(my_taps[g:g + 1, :]).astype(BF16)
-        fold = jnp.zeros((128, FILT), F32)
-        for b, count in blocks:
-            both = jnp.concatenate([circ[:count], circ[:count]], axis=1) * maskb[128 * b:128 * b + count, :]
-            window = gx[128 * b:128 * b + 256, :]
-            res = jnp.dot(both, window, preferred_element_type=F32)
-            acc[b] = jnp.where(group_of[:count] == g, res, acc[b])
-            if b < 2:
-                mine = jnp.where(group_of == g, mown[128 * b:128 * b + 128, :], jnp.zeros((), BF16))
-                prod = lax.dot_general(mine, window, (((1,), (1,)), ((), ())), preferred_element_type=F32)
-                prod = prod * maskp[128 * b:128 * b + 128, :]
-                fold = fold + prod[:, :128] + prod[:, 128:]
-        turned_back = pltpu.roll(fold, 1, 1, stride=1, stride_axis=0)
-        mix_rows.append(jnp.sum(turned_back, axis=0, keepdims=True))
+    for b in range(2):
+        for g in range(8):
+            mine = jnp.where(group_of == g, mown[128 * b:128 * b + 128, :], jnp.zeros((), BF16))
+            pairs[b, 128 * g:128 * g + 128, :] = mine
+    for b in range(2):
+        prod = lax.dot_general(pairs[b], gx[128 * b:128 * b + 256, :], (((1,), (1,)), ((), ())), preferred_element_type=F32)
+        for g in range(8):
+            part = prod[128 * g:128 * g + 128] * maskp[128 * b:128 * b + 128, :]
+            part = part[:, :128] + part[:, 128:]
+            if b == 0:
+                fold[g] = part
+            else:
+                part = pltpu.roll(part + fold[g], 1, 1, stride=1, stride_axis=0)
+                mix_rows.append(jnp.sum(part, axis=0, keepdims=True))
     for b, count in blocks:
         at = 128 * b
         back = acc[b] + skip * gx[at:at + count, :].astype(F32)
@@ -439,6 +451,9 @@
             pltpu.VMEM((WIN - 192, HALO), BF16),
             pltpu.VMEM(taps.shape, F32),
             pltpu.VMEM((4, rows, ch), BF16),
+            pltpu.VMEM((3, 1024, 256), BF16),
+            pltpu.VMEM((2, 1024, LANES), BF16),
+            pltpu.VMEM((8, 128, LANES), F32),
             pltpu.VMEM((1, LANES), I32),
             pltpu.VMEM((2 * HALO + NEAR, ch), BF16),
             pltpu.VMEM((2 * HALO + 2 * NEAR, ch), BF16),

time: 76.8 us -> 76.2 us (level)
  no operation moved by 1% of the time
where the time goes in v5:
time: 76.2 us; the launch traced here: 76 us
  Pallas kernels  74.7 us (98%)
  between operations  1.29 us (2%)
    pallas_call x1, Pallas kernels, mix_call(): pl.pallas_call(lambda *refs: mix_kernel(nz, ntp, params, *refs), grid=(st...  72.1 us
    pallas_call x1, Pallas kernels, place_call(): pl.pallas_call(place_kernel, out_shape=tuple((jax.ShapeDtypeStruct((rows,...  2.54 us

profile of v5, /device:TPU:1, one launch (start us, length us, event | category | flops | bytes accessed | tf_op | source)
XLA Modules:
  0.0 76.0 jit_solution(10138095213289587191)
XLA Ops:
  1.3 72.1 %mix.1 = (bf16[256,1024]{1,0:T(8,128)(2,1)}, bf16[256,1024]{1,0:T(8,128)(2,1)}, bf16[256,1024]{1,0:T(8,128)(2,1)}, bf16[256,1024]{1,0:T(8,128)(2,1)}, f32[16,16,128]{2,1,0:T(8,128)}) custom-call(s32[1]{0:T(128)S(6)} %copy.16.refs_0_, s32[4]{0:T(128)} %refs_1_.1, bf16[256,1024]{1,0:T(8,128)(2,1)} %refs_2_.1, bf16[256,1024]{1,0:T(8,128)(2,1)} %refs_3_.1, ...), custom_call_target="tpu_custom_call" | custom-call | tf_op jit(solution)/shard_map/mix/pallas_call | solution.py:423
  73.4 2.5 %place.1 = (bf16[256,1024]{1,0:T(8,128)(2,1)}, bf16[256,1024]{1,0:T(8,128)(2,1)}, bf16[256,1024]{1,0:T(8,128)(2,1)}, bf16[256,1024]{1,0:T(8,128)(2,1)}, f32[64,1...) custom-call(bf16[256,1024]{1,0:T(8,128)(2,1)} %get-tuple-element.19.refs_0_, ...), custom_call_target="tpu_custom_call" | custom-call | tf_op jit(solution)/shard_map/place/pallas_call | solution.py:512

commit v6 on v5

--- a/solution.py
+++ b/solution.py
@@ -191,7 +191,7 @@
 
 def mix_kernel(nz, ntp, params, fill_ref, docs_ref, q_ref, k_ref, v_ref, g_ref, ft_ref, taps_ref, skip_ref,
                ho_ref, qg_ref, kg_ref, vg_ref, pk_ref,
-               qx, kx, vx, gw, query, keys, values, qb, kb, vb, m, gx, mown, dist, near, maskf, maskb, maskp, shift, taps, vout, stack, pairs, fold,
+               qx, kx, vx, gw, query, keys, values, qb, kb, vb, m, gx, mown, dist, near, maskf, maskb, maskp, shift, taps, vout, stack, pairs, fold, circ,
                first_row, hn, hp, vbuf, tails, counts, raw, got, parts, full, squares,
                load_sem, ysend, yrecv, zsend, zrecv, hsend, hrecv, s1, r1, s2, r2, s3, r3, s4, r4):
     step = pl.program_id(0)
@@ -208,6 +208,19 @@
             m[MSLOT + OUT:, :] = jnp.zeros((m.shape[0] - MSLOT - OUT, LANES), BF16)
             gx[WIN:, :] = jnp.zeros((gx.shape[0] - WIN, LANES), BF16)
             taps[...] = taps_ref[...].astype(F32)
+            total_rows = lax.broadcasted_iota(I32, (FILT, FILT), 0) + lax.broadcasted_iota(I32, (FILT, FILT), 1)
+            reverse = (total_rows % FILT == 0).astype(F32).astype(BF16)
+
+            def filters(k, carry):
+                own = taps[pl.ds(pl.multiple_of(k * 8, 8), 8), :]
+                turned = jnp.dot(own.astype(BF16), reverse, preferred_element_type=F32)
+                for way, rows8 in enumerate((turned, own)):
+                    for g in range(8):
+                        row = jnp.broadcast_to(rows8[g:g + 1, :], (FILT, FILT))
+                        circ[way, k, g] = pltpu.roll(row, 0, 1, stride=1, stride_axis=0).astype(BF16)
+                return carry
+
+            lax.fori_loop(0, pl.num_programs(0), filters, 0)
 
         exchange(peers, fill, meanwhile, q_ref, k_ref, v_ref, g_ref, first_row, hn, hp, vbuf, tails, counts,
                  load_sem, ysend, yrecv, zsend, zrecv, hsend, hrecv)
@@ -306,22 +319,14 @@
         mown[at:at + 128, :] = jnp.dot(pick, m[MSLOT + at:MSLOT + at + 128, :], preferred_element_type=F32).astype(BF16)
 
     group_of = lax.broadcasted_iota(I32, (128, LANES), 1) // GROUP
-    my_taps = taps[pl.ds(pl.multiple_of(step * 8, 8), 8), :]
-    reverse = (lax.broadcasted_iota(I32, (FILT, FILT), 0) + lax.broadcasted_iota(I32, (FILT, FILT), 1)) % FILT == 0
-    turned = jnp.dot(my_taps.astype(BF16), reverse.astype(F32).astype(BF16), preferred_element_type=F32)
-
-    def circulant(row):
-        return pltpu.roll(jnp.broadcast_to(row, (FILT, FILT)), 0, 1, stride=1, stride_axis=0)
-
     blocks = ((0, 128), (1, 128), (2, 16))
     skip = skip_ref[:, lanes]
 
-    def banded(rows8, mask, window):
+    def banded(way, mask, window):
         for g in range(8):
-            circ = circulant(rows8[g:g + 1, :]).astype(BF16)
-            circ = jnp.concatenate([circ, circ], axis=1)
+            both = jnp.concatenate([circ[way, step, g], circ[way, step, g]], axis=1)
             for b, count in blocks:
-                stack[b, g * count:(g + 1) * count, :] = circ[:count] * mask[128 * b:128 * b + count, :]
+                stack[b, g * count:(g + 1) * count, :] = both[:count] * mask[128 * b:128 * b + count, :]
         acc = []
         for b, count in blocks:
             res = jnp.dot(stack[b, 0:8 * count, :], window[128 * b:128 * b + 256, :], preferred_element_type=F32)
@@ -331,7 +336,7 @@
             acc.append(out)
         return acc
 
-    acc = banded(turned, maskf, m)
+    acc = banded(0, maskf, m)
     for b, count in blocks:
         at = 128 * b
         gated = acc[b] + skip * m[MSLOT + at:MSLOT + at + count, :].astype(F32)
@@ -340,7 +345,7 @@
             inside = lax.broadcasted_iota(I32, (count, LANES), 0) + at < fill
             vout[0, at:at + count, lanes] = jnp.where(inside, query[at:at + count, :] * gated, 0.0).astype(BF16)
 
-    acc = banded(my_taps, maskb, gx)
+    acc = banded(1, maskb, gx)
     mix_rows = []
     for b in range(2):
         for g in range(8):
@@ -454,6 +459,7 @@
             pltpu.VMEM((3, 1024, 256), BF16),
             pltpu.VMEM((2, 1024, LANES), BF16),
             pltpu.VMEM((8, 128, LANES), F32),
+            pltpu.VMEM((2, steps, 8, FILT, FILT), BF16),
             pltpu.VMEM((1, LANES), I32),
             pltpu.VMEM((2 * HALO + NEAR, ch), BF16),
             pltpu.VMEM((2 * HALO + 2 * NEAR, ch), BF16),
@@ -477,12 +483,12 @@
 def place_kernel(*refs):
     big, pk_ref, outs, small = refs[:4], refs[4], refs[5:9], refs[9:12]
     held, pk, mix, skip, feat, load, store = refs[12:]
-    half = held.shape[1] // 2
-    moves = [(i, j, pl.ds(half * j, half)) for j in range(2) for i in range(4)]
+    part = held.shape[1] // 4
+    moves = [(i, j, pl.ds(part * j, part)) for j in range(4) for i in range(4)]
     first = pltpu.make_async_copy(pk_ref, pk, load.at[4, 0])
     first.start()
-    loads = [pltpu.make_async_copy(big[i].at[part], held.at[i, part], load.at[i, j]) for i, j, part in moves]
-    stores = [pltpu.make_async_copy(held.at[i, part], outs[i].at[part], store.at[i, j]) for i, j, part in moves]
+    loads = [pltpu.make_async_copy(big[i].at[at], held.at[i, at], load.at[i, j]) for i, j, at in moves]
+    stores = [pltpu.make_async_copy(held.at[i, at], outs[i].at[at], store.at[i, j]) for i, j, at in moves]
     for c in loads:
         c.start()
     first.wait()
@@ -517,7 +523,7 @@
         out_specs=(hbm,) * 7,
         scratch_shapes=[pltpu.VMEM((4, rows, ch), BF16), pltpu.VMEM(pk.shape, F32)]
         + [pltpu.VMEM(shape, F32) for shape in small]
-        + [pltpu.SemaphoreType.DMA((5, 2)), pltpu.SemaphoreType.DMA((7, 2))],
+        + [pltpu.SemaphoreType.DMA((5, 4)), pltpu.SemaphoreType.DMA((7, 4))],
         compiler_params=pltpu.CompilerParams(vmem_limit_bytes=60 << 20),
         name="place",
     )(*big, pk)

time: 76.2 us -> 76.3 us (level)
  no operation moved by 1% of the time
where the time goes in v6:
time: 76.3 us; the launch traced here: 76.1 us
  Pallas kernels  74.8 us (98%)
  between operations  1.29 us (2%)
    pallas_call x1, Pallas kernels, mix_call(): pl.pallas_call(lambda *refs: mix_kernel(nz, ntp, params, *refs), grid=(st...  72 us
    pallas_call x1, Pallas kernels, place_call(): pl.pallas_call(place_kernel, out_shape=tuple((jax.ShapeDtypeStruct((rows,...  2.76 us

profile of v6, /device:TPU:1, one launch (start us, length us, event | category | flops | bytes accessed | tf_op | source)
XLA Modules:
  0.0 76.1 jit_solution(10142733800469752310)
XLA Ops:
  1.3 72.0 %mix.1 = (bf16[256,1024]{1,0:T(8,128)(2,1)}, bf16[256,1024]{1,0:T(8,128)(2,1)}, bf16[256,1024]{1,0:T(8,128)(2,1)}, bf16[256,1024]{1,0:T(8,128)(2,1)}, f32[16,16,128]{2,1,0:T(8,128)}) custom-call(s32[1]{0:T(128)S(6)} %copy.16.refs_0_, s32[4]{0:T(128)} %refs_1_.1, bf16[256,1024]{1,0:T(8,128)(2,1)} %refs_2_.1, bf16[256,1024]{1,0:T(8,128)(2,1)} %refs_3_.1, ...), custom_call_target="tpu_custom_call" | custom-call | tf_op jit(solution)/shard_map/mix/pallas_call | solution.py:428
  73.3 2.8 %place.1 = (bf16[256,1024]{1,0:T(8,128)(2,1)}, bf16[256,1024]{1,0:T(8,128)(2,1)}, bf16[256,1024]{1,0:T(8,128)(2,1)}, bf16[256,1024]{1,0:T(8,128)(2,1)}, f32[64,1...) custom-call(bf16[256,1024]{1,0:T(8,128)(2,1)} %get-tuple-element.19.refs_0_, ...), custom_call_target="tpu_custom_call" | custom-call | tf_op jit(solution)/shard_map/place/pallas_call | solution.py:518
